TPU v7x, 256 devices: a whole 4x4x8 slice. The times are simulated.
256 devices in a mesh: sx: 8 (over y_lo, x), sy: 16 (over z, core), hd: 2 (over y_hi).
Axes of the slice: x: 4, y: 4 (y_hi: 2, y_lo: 2; y = y_hi * 2 + y_lo), z: 8, core: 2. Of those that a mesh axis runs over, the one named last changes fastest.
Arguments:
- queries: bfloat16 [16, 32, 12, 32, 128], P('sx', 'sy', 'hd'), may hold values from -10 to 10
- key_field: bfloat16 [16, 32, 12, 32, 128], P('sx', 'sy', 'hd'), may hold values from -10 to 10
- value_field: bfloat16 [16, 32, 12, 32, 128], P('sx', 'sy', 'hd'), may hold values from -6 to 6
- grad_output: bfloat16 [16, 32, 384, 128], P('sx', 'sy'), may hold values from -6 to 6
- out_weight: bfloat16 [384, 384], P('hd'), may hold values from -0.3125 to 0.3125
- window_counts: int32 [16, 32], P('sx', 'sy'), may hold values from 1 to 8
- adjacent: int32 [16, 32, 2], P('sx', 'sy'), may hold values from 0 to 3, all different within a row
- far_list: int32 [16, 32, 4], P('sx', 'sy'), may hold values from 0 to 15, all different within a row
Outputs:
- block_out: bfloat16 [16, 32, 384, 128], P('sx', 'sy', 'hd')
- grad_queries: bfloat16 [16, 32, 12, 32, 128], P('sx', 'sy', 'hd')
- grad_key_field: bfloat16 [16, 32, 12, 32, 128], P('sx', 'sy', 'hd')
- grad_value_field: bfloat16 [16, 32, 12, 32, 128], P('sx', 'sy', 'hd')
Inputs may be any that keep to these rules, and one draw needn't show every extreme that they name: `adjacent`: the codes of one window are distinct. `far_list`: entry e names coarse row e // 16 of the 1 coarse rows covering the window's block of 2 window rows, coarse column e % 16; the entries of one window are distinct.
All inputs are finite; a program needn't handle non-finite values.
Results may differ from a plain program's by a relative error of at most 0.012.
Values may be sent and summed in bfloat16 or wider, within the bound.
A program may use at most 128 MiB of HBM per device.

v0:
```python
import math

import jax
import jax.numpy as jnp
from jax import lax
from jax.sharding import PartitionSpec as P

PGRP = 16


def padded(cells, sides, width):
    for axis, dim in sides:
        count = lax.axis_size(axis)
        ends = count - 1
        head = lax.slice_in_dim(cells, 0, width, axis=dim)
        tail = lax.slice_in_dim(cells, cells.shape[dim] - width, cells.shape[dim], axis=dim)
        cells = jnp.concatenate(
            [
                lax.ppermute(tail, axis, [(i, (i + 1) % count) for i in range(ends)]),
                cells,
                lax.ppermute(head, axis, [((i + 1) % count, i) for i in range(ends)]),
            ],
            axis=dim,
        )
    return cells


def pool_pairs(stacked, group_size):
    grid_x, grid_y, pair_dim, head_count, head_dim, window_len = stacked.shape
    cell_count = window_len // group_size
    grouped = stacked.astype(jnp.float32).reshape(
        grid_x // 2, 2, grid_y // 2, 2, pair_dim, head_count, head_dim, cell_count, group_size
    )
    pooled = jnp.mean(grouped, axis=8)
    pooled = jnp.transpose(pooled, (0, 2, 4, 5, 6, 1, 3, 7))
    return pooled.reshape(
        grid_x // 2, grid_y // 2, pair_dim, head_count, head_dim, 4 * cell_count
    ).astype(jnp.bfloat16)


def pooled_valid(window_counts, cell_count):
    grid_x, grid_y = window_counts.shape
    quarter_counts = jnp.transpose(
        window_counts.reshape(grid_x // 2, 2, grid_y // 2, 2), (0, 2, 1, 3)
    ).reshape(grid_x // 2, grid_y // 2, 4)
    is_valid = (
        jnp.arange(cell_count, dtype=jnp.int32)[None, None, None, :] < quarter_counts[:, :, :, None]
    )
    return is_valid.reshape(grid_x // 2, grid_y // 2, 4 * cell_count).astype(jnp.int32)


def spread_pooled(grads_in, group_size):
    half_x, half_y, pair_dim, head_count, head_dim, pooled_len = grads_in.shape
    cell_count = pooled_len // 4
    split = grads_in.reshape(half_x, half_y, pair_dim, head_count, head_dim, 2, 2, cell_count)
    split = jnp.transpose(split, (0, 5, 1, 6, 2, 3, 4, 7)).reshape(
        2 * half_x, 2 * half_y, pair_dim, head_count, head_dim, cell_count
    )
    spread = jnp.broadcast_to(split[..., None], split.shape + (group_size,))
    return spread.reshape(split.shape[:5] + (cell_count * group_size,)) / group_size


def direction_steps(adjacent_row):
    step_x = (adjacent_row == 1).astype(jnp.int32) - (adjacent_row == 0).astype(jnp.int32)
    step_y = (adjacent_row == 3).astype(jnp.int32) - (adjacent_row == 2).astype(jnp.int32)
    return (step_x, step_y)


def assemble(own_part, beside, far_part, own_count, beside_count, far_mask, group_size):
    blocks = beside.shape[0]
    pair_dim, head_count, head_dim, window_len = (
        own_part.shape[1],
        own_part.shape[2],
        own_part.shape[3],
        own_part.shape[4],
    )
    beside_flat = jnp.transpose(beside, (0, 2, 3, 4, 1, 5)).reshape(
        blocks, pair_dim, head_count, head_dim, -1
    )
    far_flat = jnp.transpose(far_part, (0, 2, 3, 4, 1, 5)).reshape(
        blocks, pair_dim, head_count, head_dim, -1
    )
    joined = jnp.concatenate([own_part, beside_flat, far_flat], axis=4)
    positions = jnp.arange(window_len, dtype=jnp.int32)
    own_valid = positions[None, :] < group_size * own_count[:, None]
    beside_valid = (positions[None, None, :] < group_size * beside_count[:, :, None]).reshape(
        blocks, -1
    )
    far_valid = (far_mask > 0).reshape(blocks, -1)
    key_mask = jnp.concatenate([own_valid, beside_valid, far_valid], axis=1)
    return (joined[:, 0], joined[:, 1], key_mask)


def split_grads(grad_keys, grad_values, window_len, slot_count, far_count):
    blocks, head_count, head_dim = (grad_keys.shape[0], grad_keys.shape[1], grad_keys.shape[2])
    paired = jnp.stack([grad_keys, grad_values], axis=1)
    own_grad = paired[..., :window_len]
    near_end = window_len * (1 + slot_count)
    beside_grad = paired[..., window_len:near_end].reshape(
        blocks, 2, head_count, head_dim, slot_count, window_len
    )
    beside_grad = jnp.transpose(beside_grad, (0, 4, 1, 2, 3, 5))
    far_grad = paired[..., near_end:].reshape(blocks, 2, head_count, head_dim, far_count, -1)
    far_grad = jnp.transpose(far_grad, (0, 4, 1, 2, 3, 5))
    return (own_grad, beside_grad, far_grad)


def window_pass(query_rows, grad_rows, key_block, value_block, key_mask, query_mask):
    score_scale = 1.0 / math.sqrt(query_rows.shape[2])
    scores = (
        jnp.einsum("bhdi,bhdj->bhij", query_rows, key_block, preferred_element_type=jnp.float32)
        * score_scale
    )
    scores = jnp.where(key_mask[:, None, None, :], scores, -jnp.inf)
    row_max = jnp.max(scores, axis=3, keepdims=True)
    exponent = jnp.exp(scores - row_max)
    weights = exponent / jnp.sum(exponent, axis=3, keepdims=True)
    weights_low = weights.astype(jnp.bfloat16)
    attended = jnp.einsum(
        "bhij,bhdj->bhdi", weights_low, value_block, preferred_element_type=jnp.float32
    )
    attended = jnp.where(query_mask[:, None, None, :], attended, 0.0).astype(jnp.bfloat16)
    grad_prob = jnp.einsum(
        "bhdi,bhdj->bhij", grad_rows, value_block, preferred_element_type=jnp.float32
    )
    centre = jnp.sum(weights * grad_prob, axis=3, keepdims=True)
    grad_score = (weights * (grad_prob - centre) * score_scale).astype(jnp.bfloat16)
    grad_query = jnp.einsum(
        "bhij,bhdj->bhdi", grad_score, key_block, preferred_element_type=jnp.float32
    )
    grad_keys = jnp.einsum(
        "bhij,bhdi->bhdj", grad_score, query_rows, preferred_element_type=jnp.float32
    )
    grad_values = jnp.einsum(
        "bhij,bhdi->bhdj", weights_low, grad_rows, preferred_element_type=jnp.float32
    )
    return (attended, grad_query, grad_keys, grad_values)


def local(
    queries, key_field, value_field, grad_output, out_weight, window_counts, adjacent, far_list
):
    per_side, head_count, head_dim, window_len = (
        queries.shape[0],
        queries.shape[2],
        queries.shape[3],
        queries.shape[4],
    )
    cell_count = window_len // PGRP
    stacked = jnp.stack([key_field, value_field], axis=2)
    stacked_ext, counts_ext = (
        padded(stacked, (("sx", 0), ("sy", 1)), 1),
        padded(window_counts, (("sx", 0), ("sy", 1)), 1),
    )
    pooled = pool_pairs(stacked, PGRP)
    pooled_mask = pooled_valid(window_counts, cell_count)
    strip_kv, strip_mask = (
        lax.all_gather(pooled, "sy", axis=1, tiled=True),
        lax.all_gather(pooled_mask, "sy", axis=1, tiled=True),
    )
    strip_kv = strip_kv.reshape((-1,) + strip_kv.shape[2:])
    strip_mask = strip_mask.reshape((-1,) + strip_mask.shape[2:])
    positions = jnp.arange(window_len, dtype=jnp.int32)
    query_valid = positions[None, None, :] < PGRP * window_counts[:, :, None]
    grad_mixed = jnp.einsum(
        "fc,abci->abfi", out_weight, grad_output, preferred_element_type=jnp.float32
    )
    grad_mixed = jnp.where(query_valid[:, :, None, :], grad_mixed, 0.0).astype(jnp.bfloat16)
    grad_mixed = grad_mixed.reshape(queries.shape)
    columns = jnp.arange(per_side, dtype=jnp.int32)

    def row_step(state_in, inputs):
        ext_grads, strip_grads = state_in
        row_index, query_row, grad_row, adjacent_row, far_row, count_row = inputs
        step_x, step_y = direction_steps(adjacent_row)
        near_x = row_index + 1 + step_x
        near_y = columns[:, None] + 1 + step_y
        own_part = lax.dynamic_index_in_dim(stacked_ext, row_index + 1, 0, keepdims=False)[
            1 : per_side + 1
        ]
        beside = stacked_ext[near_x, near_y]
        beside_count = counts_ext[near_x, near_y]
        far_part = strip_kv[far_row]
        far_mask = strip_mask[far_row]
        key_block, value_block, key_mask = assemble(
            own_part, beside, far_part, count_row, beside_count, far_mask, PGRP
        )
        query_mask = positions[None, :] < PGRP * count_row[:, None]
        attended, grad_query, grad_keys, grad_values = window_pass(
            query_row, grad_row, key_block, value_block, key_mask, query_mask
        )
        own_grad, beside_grad, far_grad = split_grads(
            grad_keys, grad_values, window_len, beside.shape[1], far_row.shape[1]
        )
        ext_grads = ext_grads.at[row_index + 1, 1 : per_side + 1].add(own_grad)
        ext_grads = ext_grads.at[near_x, near_y].add(beside_grad)
        strip_grads = strip_grads.at[far_row].add(far_grad)
        return ((ext_grads, strip_grads), (attended, grad_query.astype(jnp.bfloat16)))

    start_state = (
        jnp.zeros(stacked_ext.shape, jnp.float32),
        jnp.zeros(strip_kv.shape, jnp.float32),
    )
    row_inputs = (
        jnp.arange(per_side, dtype=jnp.int32),
        queries,
        grad_mixed,
        adjacent,
        far_list,
        window_counts,
    )
    (ext_grads, strip_grads), (attended, grad_queries) = lax.scan(row_step, start_state, row_inputs)
    rest_shape = ext_grads.shape[2:]
    half_side = per_side // 2
    x_rims = jnp.stack([ext_grads[0, 1:-1], ext_grads[-1, 1:-1]])
    y_rims = jnp.stack([ext_grads[1:-1, 0], ext_grads[1:-1, -1]])
    x_parts = x_rims.reshape((2, 2, half_side) + rest_shape)
    y_parts = jnp.swapaxes(y_rims.reshape((2, 2, half_side) + rest_shape), 0, 1)
    packed_rims = jnp.stack([x_parts, y_parts], axis=2)
    received = padded(packed_rims.astype(jnp.bfloat16), (("sx", 0), ("sy", 1)), 1).astype(
        packed_rims.dtype
    )
    from_x_lower = received[0, 1:3, 0].reshape((per_side,) + rest_shape)
    from_x_upper = received[3, 1:3, 0].reshape((per_side,) + rest_shape)
    from_y_lower = received[1:3, 0, 1].reshape((per_side,) + rest_shape)
    from_y_upper = received[1:3, 3, 1].reshape((per_side,) + rest_shape)
    near_grads = ext_grads[1:-1, 1:-1]
    near_grads = near_grads.at[0].add(from_x_lower).at[-1].add(from_x_upper)
    near_grads = near_grads.at[:, 0].add(from_y_lower).at[:, -1].add(from_y_upper)
    strip_grads = strip_grads.reshape((half_side, -1) + strip_grads.shape[1:])
    own_coarse = lax.psum_scatter(
        strip_grads.astype(jnp.bfloat16), "sy", scatter_dimension=1, tiled=True
    ).astype(jnp.float32)
    totals = near_grads + spread_pooled(own_coarse, PGRP)
    flat_out = attended.reshape(per_side, per_side, head_count * head_dim, window_len)
    partial_mix = jnp.einsum(
        "abfi,fc->abci", flat_out, out_weight, preferred_element_type=jnp.float32
    )
    block_out = lax.psum_scatter(
        partial_mix.astype(jnp.bfloat16), "hd", scatter_dimension=2, tiled=True
    )
    return (
        block_out,
        grad_queries,
        totals[:, :, 0].astype(jnp.bfloat16),
        totals[:, :, 1].astype(jnp.bfloat16),
    )


def solution(mesh):
    in_specs = (
        P("sx", "sy", "hd", None, None),
        P("sx", "sy", "hd", None, None),
        P("sx", "sy", "hd", None, None),
        P("sx", "sy", None, None),
        P("hd", None),
        P("sx", "sy"),
        P("sx", "sy", None),
        P("sx", "sy", None),
    )
    out_specs = (
        P("sx", "sy", "hd", None),
        P("sx", "sy", "hd", None, None),
        P("sx", "sy", "hd", None, None),
        P("sx", "sy", "hd", None, None),
    )
    return jax.shard_map(local, mesh=mesh, in_specs=in_specs, out_specs=out_specs, check_vma=False)
```

profile of v0, /device:TPU:1, one launch (start us, length us, event | category | flops | bytes accessed | tf_op | source)
XLA Modules:
  0.0 330.9 jit_solution(11693680826515756934)
XLA Ops:
  9.2 4.0 %collective-permute-start.4 = (bf16[1,2,2,6,32,128]{5,4,3,1,2,0:T(8,128)(2,1)S(1)}, bf16[1,2,2,6,32,128]{5,4,3,1,2,0:T(8,128)(2,1)S(1)}, u32[]{:S(2)}, u32[]{:S(2)}) collective-permute-start(bf16[1,2,2,6,32,128]{5,4,3,1,2,0:T(8,128)(2,1)S(1)} %get-tuple-element.468), channel_id=1, source_target_pairs={{0,32},{32,64},{64,96},{96,128},{128,160},{160,192},{192,224},{1,3... | collective-permute-start | bytes 589832 | tf_op jit(solution)/shard_map/ppermute | solution.py:19
  15.7 4.0 %collective-permute-start = (s32[1,2]{1,0:T(1,128)}, s32[1,2]{1,0:T(1,128)S(1)}, u32[]{:S(2)}, u32[]{:S(2)}) collective-permute-start(s32[1,2]{1,0:T(1,128)} %get-tuple-element.472), channel_id=1, source_target_pairs={{0,32},{32,64},{64,96},{96,128},{128,160},{160,192},{192,224},{1,3... | collective-permute-start | bytes 32 | tf_op jit(solution)/shard_map/ppermute | solution.py:19
  27.4 21.2 %all_gather.6 = s32[1,16,32]{2,0,1:T(1,128)S(1)} all-gather(s32[1,1,32]{2,0,1:T(1,128)S(1)} %fusion.88), channel_id=1, replica_groups=mesh['sx'=8,'sy'=16,'hd'=2] {'sy'}, dimensions={1}, use_global_device_ids=true | all-gather | bytes 2176 | tf_op jit(solution)/shard_map/all_gather | solution.py:159
  48.5 20.8 %all_gather.7 = bf16[1,16,2,6,32,32]{5,4,3,2,0,1:T(8,128)(2,1)} all-gather(bf16[1,1,2,6,32,32]{5,4,3,2,0,1:T(8,128)(2,1)S(1)} %copy.108), channel_id=1, replica_groups=mesh['sx'=8,'sy'=16,'hd'=2] {'sy'}, dimensions={1}, use_global_device_ids=true | all-gather | bytes 417792 | tf_op jit(solution)/shard_map/all_gather | solution.py:158
  69.6 3.1 collective-permute-start.6
  75.4 3.6 %collective-permute-start.2 = (s32[4,1]{1,0:T(4,128)S(1)}, s32[4,1]{1,0:T(4,128)S(1)}, u32[]{:S(2)}, u32[]{:S(2)}) collective-permute-start(s32[4,1]{1,0:T(4,128)S(1)} %get-tuple-element.470), channel_id=1, source_target_pairs={{0,2},{2,4},{4,6},{6,8},{8,10},{10,12},{12,14},{14,16},{16,18},{18... | collective-permute-start | bytes 56 | tf_op jit(solution)/shard_map/ppermute | solution.py:19
  81.2 2.8 collective-permute-done.3
  88.7 2.1 broadcast_in_dim.127
  90.8 141.3 %while.26 = (s32[]{:T(128)}, f32[4,4,2,6,32,128]{5,4,3,2,1,0:T(8,128)}, f32[16,2,6,32,32]{4,3,2,1,0:T(8,128)}, bf16[2,2,6,32,128]{4,3,2,1,0:T(8,128)(2,1)}, bf16...) while((s32[]{:T(128)}, ...), condition=%wide.region_8.9_spmd.clone.clone, body=%wide.region_1.8_spmd.clone.clone.sunk | while | flops 324829888 | bytes 90168096 | solution.py:212
  113.8 3.1 fusion.138
  119.2 12.0 %fusion.144 = bf16[2,2,6,32,128]{4,3,2,1,0:T(8,128)(2,1)} fusion(bf16[2,2,6,32,128]{4,3,2,1,0:T(8,128)(2,1)} %get-tuple-element.609, s32[]{:T(128)} %get-tuple-element.605, f32[2,6,128,512]{3,2,1,0:T(8,128)S(1)} %fusion.135, bf16[2,2,6,32,512]{4,3,2,0,1:T(8,128)(2,1)} %copy-done.3, f32[2,6,128,512]{3,2,1,0:T(8,128)} %get-tuple-element.575, ...), kind=kOutput, calls=%fused_computation.43.clone.1 | convolution fusion | flops 55887872 | bytes 13091328 | tf_op jit(solution)/shard_map/while/body/eval_jaxpr/bhij,bhdj->bhdi/dot_general | solution.py:128
  131.2 2.3 convolution_bitcast_fusion.2
  133.5 12.8 %fusion.139 = f32[2,1,6,32,512]{4,3,2,0,1:T(8,128)S(1)} fusion(f32[2,6,128,512]{3,2,1,0:T(8,128)} %copy-done.2, bf16[2,2,6,32,128]{4,3,2,1,0:T(8,128)(2,1)S(1)} %copy-done.16, s32[]{:T(128)} %get-tuple-element.605, f32[2,6,128,512]{3,2,1,0:T(8,128)} %get-tuple-element.575, f32[2,6,128]{2,1,0:T(8,128)S(1)} %copy-done.27), kind=kOutput, calls=%fused_computation.38.clone.1 | convolution fusion | flops 55838720 | bytes 13484544 | tf_op jit(solution)/shard_map/while/body/eval_jaxpr/bhij,bhdi->bhdj/dot_general | solution.py:131
  147.3 3.9 %scatter_fusion.1 = f32[16,2,6,32,32]{4,3,2,1,0:T(8,128)} fusion(f32[16,2,6,32,32]{4,3,2,1,0:T(8,128)} %get-tuple-element.607, s32[8]{0:T(128)S(1)} %copy-done.22, f32[8,2,6,32,32]{4,3,2,1,0:T(8,128)S(1)} %bitcast.243), kind=kCustom, calls=%fused_computation.5.clone.clone.1 | custom fusion | flops 98304 | bytes 1179680 | tf_op jit(solution)/shard_map/while/body/eval_jaxpr/scatter-add | solution.py:197
  151.2 3.3 %fusion.143 = bf16[2,2,6,32,128]{4,3,2,1,0:T(8,128)(2,1)} fusion(bf16[2,2,6,32,128]{4,3,2,1,0:T(8,128)(2,1)} %get-tuple-element.608, s32[]{:T(128)} %get-tuple-element.605, bf16[2,2,6,32,512]{4,3,2,0,1:T(8,128)(2,1)} %copy-done.3, pred[2,128]{1,0:T(4,128)(4,1)} %copy-done.24, f32[2,6,128,512]{3,2,1,0:T(8,128)} %get-tuple-element.575, ...), kind=kOutput, calls=%fused_computation.45.clone.1 | convolution fusion | flops 52002816 | bytes 3646464 | tf_op jit(solution)/shard_map/while/body/eval_jaxpr/bhij,bhdj->bhdi/dot_general | solution.py:119
  155.8 2.5 copy_dynamic-update-slice_fusion.2
  158.4 3.0 scatter_fusion
  184.4 3.1 fusion.138
  189.8 12.0 %fusion.144 = bf16[2,2,6,32,128]{4,3,2,1,0:T(8,128)(2,1)} fusion(bf16[2,2,6,32,128]{4,3,2,1,0:T(8,128)(2,1)} %get-tuple-element.609, s32[]{:T(128)} %get-tuple-element.605, f32[2,6,128,512]{3,2,1,0:T(8,128)S(1)} %fusion.135, bf16[2,2,6,32,512]{4,3,2,0,1:T(8,128)(2,1)} %copy-done.3, f32[2,6,128,512]{3,2,1,0:T(8,128)} %get-tuple-element.575, ...), kind=kOutput, calls=%fused_computation.43.clone.1 | convolution fusion | flops 55887872 | bytes 13091328 | tf_op jit(solution)/shard_map/while/body/eval_jaxpr/bhij,bhdj->bhdi/dot_general | solution.py:128
  201.8 2.3 convolution_bitcast_fusion.2
  204.1 12.8 %fusion.139 = f32[2,1,6,32,512]{4,3,2,0,1:T(8,128)S(1)} fusion(f32[2,6,128,512]{3,2,1,0:T(8,128)} %copy-done.2, bf16[2,2,6,32,128]{4,3,2,1,0:T(8,128)(2,1)S(1)} %copy-done.16, s32[]{:T(128)} %get-tuple-element.605, f32[2,6,128,512]{3,2,1,0:T(8,128)} %get-tuple-element.575, f32[2,6,128]{2,1,0:T(8,128)S(1)} %copy-done.27), kind=kOutput, calls=%fused_computation.38.clone.1 | convolution fusion | flops 55838720 | bytes 13484544 | tf_op jit(solution)/shard_map/while/body/eval_jaxpr/bhij,bhdi->bhdj/dot_general | solution.py:131
  217.9 4.0 %scatter_fusion.1 = f32[16,2,6,32,32]{4,3,2,1,0:T(8,128)} fusion(f32[16,2,6,32,32]{4,3,2,1,0:T(8,128)} %get-tuple-element.607, s32[8]{0:T(128)S(1)} %copy-done.22, f32[8,2,6,32,32]{4,3,2,1,0:T(8,128)S(1)} %bitcast.243), kind=kCustom, calls=%fused_computation.5.clone.clone.1 | custom fusion | flops 98304 | bytes 1179680 | tf_op jit(solution)/shard_map/while/body/eval_jaxpr/scatter-add | solution.py:197
  221.9 3.3 %fusion.143 = bf16[2,2,6,32,128]{4,3,2,1,0:T(8,128)(2,1)} fusion(bf16[2,2,6,32,128]{4,3,2,1,0:T(8,128)(2,1)} %get-tuple-element.608, s32[]{:T(128)} %get-tuple-element.605, bf16[2,2,6,32,512]{4,3,2,0,1:T(8,128)(2,1)} %copy-done.3, pred[2,128]{1,0:T(4,128)(4,1)} %copy-done.24, f32[2,6,128,512]{3,2,1,0:T(8,128)} %get-tuple-element.575, ...), kind=kOutput, calls=%fused_computation.45.clone.1 | convolution fusion | flops 52002816 | bytes 3646464 | tf_op jit(solution)/shard_map/while/body/eval_jaxpr/bhij,bhdj->bhdi/dot_general | solution.py:119
  226.5 2.5 copy_dynamic-update-slice_fusion.2
  229.1 3.0 scatter_fusion
  232.1 2.3 convert.22
  236.3 4.9 %collective-permute-start.8 = (bf16[1,2,2,1,2,6,32,128]{7,6,5,4,3,2,1,0:T(8,128)(2,1)}, bf16[1,2,2,1,2,6,32,128]{7,6,5,4,3,2,1,0:T(8,128)(2,1)}, u32[]{:S(2)}, u32[]{:S(2)}) collective-permute-start(bf16[1,2,2,1,2,6,32,128]{7,6,5,4,3,2,1,0:T(8,128)(2,1)} %get-tuple-element.462), channel_id=1, source_target_pairs={{0,32},{32,64},{64,96},{96,128},{128,160},{160,192},{192,224},{1,3... | collective-permute-start | bytes 1179656 | tf_op jit(solution)/shard_map/ppermute | solution.py:19
  248.3 8.0 %collective-permute-done.9 = bf16[1,2,2,1,2,6,32,128]{7,6,5,4,3,2,1,0:T(8,128)(2,1)} collective-permute-done((bf16[1,2,2,1,2,6,32,128]{7,6,5,4,3,2,1,0:T(8,128)(2,1)}, bf16[1,2,2,1,2,6,32,128]{7,6,5,4,3,2,1,0:T(8,128)(2,1)}, u32[]{:S(2)}, u32[]{:S(2)}) %collective-permute-start.9) | collective-permute-done | bytes 393248 | tf_op jit(solution)/shard_map/ppermute | solution.py:21
  259.6 3.4 %collective-permute-start.10 = (bf16[4,1,2,1,2,6,32,128]{7,6,5,4,3,2,1,0:T(8,128)(2,1)}, bf16[4,1,2,1,2,6,32,128]{7,6,5,4,3,2,1,0:T(8,128)(2,1)}, u32[]{:S(2)}, u32[]{:S(2)}) collective-permute-start(bf16[4,1,2,1,2,6,32,128]{7,6,5,4,3,2,1,0:T(8,128)(2,1)} %get-tuple-element.456), channel_id=1, source_target_pairs={{0,2},{2,4},{4,6},{6,8},{8,10},{10,12},{12,14},{14,16},{16,18},{18... | collective-permute-start | bytes 2359304 | tf_op jit(solution)/shard_map/ppermute | solution.py:19
  267.5 18.7 %all-reduce.3.cloned.1.call-done = bf16[2,2,384,128]{3,1,0,2:T(2,128)(2,1)} async-done(((bf16[2,2,384,128]{3,1,0,2:T(2,128)(2,1)}), bf16[2,2,384,128]{3,1,0,2:T(2,128)(2,1)}) %all-reduce.3.cloned.1.call-update) | async-done | bytes 393232
  287.9 19.4 %reduce-scatter.2.cloned.1.call-done = bf16[1,1,2,6,32,32]{4,5,3,2,1,0:T(8,128)(2,1)} async-done(((bf16[1,16,2,6,32,32]{4,5,3,2,1,0:T(8,128)(2,1)}), bf16[1,1,2,6,32,32]{4,5,3,2,1,0:T(8,128)(2,1)}) %reduce-scatter.2.cloned.1.call-update) | async-done | bytes 24592 | tf_op jit(solution)/shard_map/reduce_scatter | solution.py:231
  310.1 3.1 copy.119
  (230 shorter events, 104.0 us)
Async XLA Ops:
  8.0 18.3 %copy-start = (bf16[2,2,384,128]{3,2,1,0:T(8,128)(2,1)S(1)}, bf16[2,2,384,128]{3,2,1,0:T(8,128)(2,1)}, u32[]{:S(2)}) copy-start(bf16[2,2,384,128]{3,2,1,0:T(8,128)(2,1)} %param.23) | copy-start | bytes 1179652
  8.0 18.2 %copy-start.17 = (bf16[192,384]{1,0:T(8,128)(2,1)S(1)}, bf16[192,384]{1,0:T(8,128)(2,1)}, u32[]{:S(2)}) copy-start(bf16[192,384]{1,0:T(8,128)(2,1)} %param.24) | copy-start | bytes 442372
  8.0 278.1 %all-reduce.3.cloned.1.call-start = ((), (), s32[]{:S(2)}) async-start(), calls=%async_computation.2 | async-start | bytes 786432
  9.2 60.2 %collective-permute-start.4 = (bf16[1,2,2,6,32,128]{5,4,3,1,2,0:T(8,128)(2,1)S(1)}, bf16[1,2,2,6,32,128]{5,4,3,1,2,0:T(8,128)(2,1)S(1)}, u32[]{:S(2)}, u32[]{:S(2)}) collective-permute-start(bf16[1,2,2,6,32,128]{5,4,3,1,2,0:T(8,128)(2,1)S(1)} %get-tuple-element.468), channel_id=1, source_target_pairs={{0,32},{32,64},{64,96},{96,128},{128,160},{160,192},{192,224},{1,3... | collective-permute-start | bytes 589832 | tf_op jit(solution)/shard_map/ppermute | solution.py:19
  13.2 56.2 %collective-permute-start.5 = (bf16[1,2,2,6,32,128]{5,4,3,1,2,0:T(8,128)(2,1)S(1)}, bf16[1,2,2,6,32,128]{5,4,3,1,2,0:T(8,128)(2,1)S(1)}, u32[]{:S(2)}, u32[]{:S(2)}) collective-permute-start(bf16[1,2,2,6,32,128]{5,4,3,1,2,0:T(8,128)(2,1)S(1)} %get-tuple-element.469), channel_id=1, source_target_pairs={{32,0},{64,32},{96,64},{128,96},{160,128},{192,160},{224,192},{33,... | collective-permute-start | bytes 589832 | tf_op jit(solution)/shard_map/ppermute | solution.py:21
  15.7 58.9 %collective-permute-start = (s32[1,2]{1,0:T(1,128)}, s32[1,2]{1,0:T(1,128)S(1)}, u32[]{:S(2)}, u32[]{:S(2)}) collective-permute-start(s32[1,2]{1,0:T(1,128)} %get-tuple-element.472), channel_id=1, source_target_pairs={{0,32},{32,64},{64,96},{96,128},{128,160},{160,192},{192,224},{1,3... | collective-permute-start | bytes 32 | tf_op jit(solution)/shard_map/ppermute | solution.py:19
  19.7 54.9 %collective-permute-start.1 = (s32[1,2]{1,0:T(1,128)S(1)}, s32[1,2]{1,0:T(1,128)}, u32[]{:S(2)}, u32[]{:S(2)}) collective-permute-start(s32[1,2]{1,0:T(1,128)S(1)} %get-tuple-element.473), channel_id=1, source_target_pairs={{32,0},{64,32},{96,64},{128,96},{160,128},{192,160},{224,192},{33,... | collective-permute-start | bytes 32 | tf_op jit(solution)/shard_map/ppermute | solution.py:21
  22.3 47.1 %copy-start.12 = (bf16[2,2,6,32,128]{4,3,2,1,0:T(8,128)(2,1)S(1)}, bf16[2,2,6,32,128]{4,3,2,1,0:T(8,128)(2,1)}, u32[]{:S(2)}) copy-start(bf16[2,2,6,32,128]{4,3,2,1,0:T(8,128)(2,1)} %param.21) | copy-start | bytes 589828
  22.3 47.0 %copy-start.13 = (bf16[2,2,6,32,128]{4,3,2,1,0:T(8,128)(2,1)S(1)}, bf16[2,2,6,32,128]{4,3,2,1,0:T(8,128)(2,1)}, u32[]{:S(2)}) copy-start(bf16[2,2,6,32,128]{4,3,2,1,0:T(8,128)(2,1)} %param.22) | copy-start | bytes 589828
  69.6 15.2 %collective-permute-start.6 = (bf16[4,1,2,6,32,128]{5,4,3,1,2,0:T(8,128)(2,1)S(1)}, bf16[4,1,2,6,32,128]{5,4,3,1,2,0:T(8,128)(2,1)S(1)}, u32[]{:S(2)}, u32[]{:S(2)}) collective-permute-start(bf16[4,1,2,6,32,128]{5,4,3,1,2,0:T(8,128)(2,1)S(1)} %get-tuple-element.464), channel_id=1, source_target_pairs={{0,2},{2,4},{4,6},{6,8},{8,10},{10,12},{12,14},{14,16},{16,18},{18... | collective-permute-start | bytes 1179656 | tf_op jit(solution)/shard_map/ppermute | solution.py:19
  72.7 12.0 %collective-permute-start.7 = (bf16[4,1,2,6,32,128]{5,4,3,1,2,0:T(8,128)(2,1)S(1)}, bf16[4,1,2,6,32,128]{5,4,3,1,2,0:T(8,128)(2,1)S(1)}, u32[]{:S(2)}, u32[]{:S(2)}) collective-permute-start(bf16[4,1,2,6,32,128]{5,4,3,1,2,0:T(8,128)(2,1)S(1)} %get-tuple-element.465), channel_id=1, source_target_pairs={{2,0},{4,2},{6,4},{8,6},{10,8},{12,10},{14,12},{16,14},{18,16},{20... | collective-permute-start | bytes 1179656 | tf_op jit(solution)/shard_map/ppermute | solution.py:21
  75.4 5.7 %collective-permute-start.2 = (s32[4,1]{1,0:T(4,128)S(1)}, s32[4,1]{1,0:T(4,128)S(1)}, u32[]{:S(2)}, u32[]{:S(2)}) collective-permute-start(s32[4,1]{1,0:T(4,128)S(1)} %get-tuple-element.470), channel_id=1, source_target_pairs={{0,2},{2,4},{4,6},{6,8},{8,10},{10,12},{12,14},{14,16},{16,18},{18... | collective-permute-start | bytes 56 | tf_op jit(solution)/shard_map/ppermute | solution.py:19
  79.1 4.9 %collective-permute-start.3 = (s32[4,1]{1,0:T(4,128)S(1)}, s32[4,1]{1,0:T(4,128)S(1)}, u32[]{:S(2)}, u32[]{:S(2)}) collective-permute-start(s32[4,1]{1,0:T(4,128)S(1)} %get-tuple-element.471), channel_id=1, source_target_pairs={{2,0},{4,2},{6,4},{8,6},{10,8},{12,10},{14,12},{16,14},{18,16},{20... | collective-permute-start | bytes 56 | tf_op jit(solution)/shard_map/ppermute | solution.py:21
  100.5 3.3 copy-start.21
  113.8 3.1 copy-start.4
  113.8 3.1 copy-start.15
  154.7 3.7 %copy-start.23 = (s32[2,2,1]{1,0,2:T(2,128)S(1)}, s32[2,2,1]{1,0,2:T(2,128)}, u32[]{:S(2)}) copy-start(s32[2,2,1]{1,0,2:T(2,128)} %get-tuple-element.577) | copy-start | bytes 52 | tf_op jit(solution)/shard_map/while
  171.1 3.3 copy-start.21
  184.4 3.1 copy-start.4
  184.4 3.1 copy-start.15
  225.3 3.7 %copy-start.23 = (s32[2,2,1]{1,0,2:T(2,128)S(1)}, s32[2,2,1]{1,0,2:T(2,128)}, u32[]{:S(2)}) copy-start(s32[2,2,1]{1,0,2:T(2,128)} %get-tuple-element.577) | copy-start | bytes 52 | tf_op jit(solution)/shard_map/while
  234.4 6.8 %copy-start.18 = (bf16[192,384]{1,0:T(8,128)(2,1)S(1)}, bf16[192,384]{1,0:T(8,128)(2,1)}, u32[]{:S(2)}) copy-start(bf16[192,384]{1,0:T(8,128)(2,1)} %param.24) | copy-start | bytes 442372
  234.4 6.8 %copy-start.20 = (bf16[2,2,6,32,128]{4,3,2,1,0:T(8,128)(2,1)S(1)}, bf16[2,2,6,32,128]{4,3,2,1,0:T(8,128)(2,1)}, u32[]{:S(2)}) copy-start(bf16[2,2,6,32,128]{4,3,2,1,0:T(8,128)(2,1)} %get-tuple-element.310) | copy-start | bytes 589828
  234.4 11.2 %copy-start.5 = (f32[16,2,6,32,32]{4,3,2,1,0:T(8,128)S(1)}, f32[16,2,6,32,32]{4,3,2,1,0:T(8,128)}, u32[]{:S(2)}) copy-start(f32[16,2,6,32,32]{4,3,2,1,0:T(8,128)} %get-tuple-element.313) | copy-start | bytes 2359300
  236.3 12.0 %collective-permute-start.8 = (bf16[1,2,2,1,2,6,32,128]{7,6,5,4,3,2,1,0:T(8,128)(2,1)}, bf16[1,2,2,1,2,6,32,128]{7,6,5,4,3,2,1,0:T(8,128)(2,1)}, u32[]{:S(2)}, u32[]{:S(2)}) collective-permute-start(bf16[1,2,2,1,2,6,32,128]{7,6,5,4,3,2,1,0:T(8,128)(2,1)} %get-tuple-element.462), channel_id=1, source_target_pairs={{0,32},{32,64},{64,96},{96,128},{128,160},{160,192},{192,224},{1,3... | collective-permute-start | bytes 1179656 | tf_op jit(solution)/shard_map/ppermute | solution.py:19
  244.3 63.0 %reduce-scatter.2.cloned.1.call-start = ((), (), s32[]{:S(2)}) async-start(), calls=%async_computation.1 | async-start | bytes 1671168 | tf_op jit(solution)/shard_map/reduce_scatter | solution.py:231
  244.3 12.0 %collective-permute-start.9 = (bf16[1,2,2,1,2,6,32,128]{7,6,5,4,3,2,1,0:T(8,128)(2,1)}, bf16[1,2,2,1,2,6,32,128]{7,6,5,4,3,2,1,0:T(8,128)(2,1)}, u32[]{:S(2)}, u32[]{:S(2)}) collective-permute-start(bf16[1,2,2,1,2,6,32,128]{7,6,5,4,3,2,1,0:T(8,128)(2,1)} %get-tuple-element.463), channel_id=1, source_target_pairs={{32,0},{64,32},{96,64},{128,96},{160,128},{192,160},{224,192},{33,... | collective-permute-start | bytes 1179656 | tf_op jit(solution)/shard_map/ppermute | solution.py:21
  247.4 17.5 %copy-start.25 = (u32[256]{0:T(256)S(1)}, u32[256]{0:T(256)}, u32[]{:S(2)}) copy-start(u32[256]{0:T(256)} %constant.322) | copy-start | bytes 3076
  247.4 18.8 %copy-start.1 = (f32[4,4,2,6,32,128]{5,4,3,2,1,0:T(8,128)S(1)}, f32[4,4,2,6,32,128]{5,4,3,2,1,0:T(8,128)}, u32[]{:S(2)}) copy-start(f32[4,4,2,6,32,128]{5,4,3,2,1,0:T(8,128)} %get-tuple-element.312) | copy-start | bytes 9437188
  259.6 53.6 %collective-permute-start.10 = (bf16[4,1,2,1,2,6,32,128]{7,6,5,4,3,2,1,0:T(8,128)(2,1)}, bf16[4,1,2,1,2,6,32,128]{7,6,5,4,3,2,1,0:T(8,128)(2,1)}, u32[]{:S(2)}, u32[]{:S(2)}) collective-permute-start(bf16[4,1,2,1,2,6,32,128]{7,6,5,4,3,2,1,0:T(8,128)(2,1)} %get-tuple-element.456), channel_id=1, source_target_pairs={{0,2},{2,4},{4,6},{6,8},{8,10},{10,12},{12,14},{14,16},{16,18},{18... | collective-permute-start | bytes 2359304 | tf_op jit(solution)/shard_map/ppermute | solution.py:19
  263.0 50.2 %collective-permute-start.11 = (bf16[4,1,2,1,2,6,32,128]{7,6,5,4,3,2,1,0:T(8,128)(2,1)}, bf16[4,1,2,1,2,6,32,128]{7,6,5,4,3,2,1,0:T(8,128)(2,1)}, u32[]{:S(2)}, u32[]{:S(2)}) collective-permute-start(bf16[4,1,2,1,2,6,32,128]{7,6,5,4,3,2,1,0:T(8,128)(2,1)} %get-tuple-element.457), channel_id=1, source_target_pairs={{2,0},{4,2},{6,4},{8,6},{10,8},{12,10},{14,12},{16,14},{18,16},{20... | collective-permute-start | bytes 2359304 | tf_op jit(solution)/shard_map/ppermute | solution.py:21
  316.9 3.8 %copy-start.14 = (f32[2,2,2,6,32,128]{5,4,3,2,0,1:T(8,128)S(1)}, f32[2,2,2,6,32,128]{5,4,3,2,0,1:T(8,128)}, u32[]{:S(2)}) copy-start(f32[2,2,2,6,32,128]{5,4,3,2,0,1:T(8,128)} %copy.119) | copy-start | bytes 2359300
  (22 other events, 32.4 us)
Sparse Core Ops, SparseCore 0:
  244.4 41.6 all-reduce.2
Sparse Core Ops, SparseCore 1:
  247.5 59.7 reduce-scatter.1
where the time goes:
time: 334 us; the launch traced here: 331 us
  matrix products  67.2 us (20%)
  other arithmetic  62.2 us (19%)
  local copies, waits for them, and re-layouts  57.2 us (17%)
  waiting for transfers between devices  49.7 us (15%)
  blocking collectives  42 us (13%)
  starting transfers between devices  32.9 us (10%)
  between operations  16.6 us (5%)
    dot_general x2, matrix products, window_pass(): jnp.einsum('bhij,bhdi->bhdj', grad_score, query_rows, preferred_element_t...  25.7 us
    dot_general x2, matrix products, window_pass(): jnp.einsum('bhij,bhdj->bhdi', grad_score, key_block, preferred_element_ty...  23.9 us
    ppermute x6, starting transfers between devices, padded(): lax.ppermute(tail, axis, [(i, (i + 1) % count) for i in range(ends)])  23 us
    all_gather x1, blocking collectives, local(): lax.all_gather(pooled_mask, 'sy', axis=1, tiled=True)  21.2 us
    all_gather x1, blocking collectives, local(): lax.all_gather(pooled, 'sy', axis=1, tiled=True)  20.8 us
    reduce_scatter x1, waiting for transfers between devices, local(): lax.psum_scatter(strip_grads.astype(jnp.bfloat16), 'sy', scatter_dimensio...  19.4 us
    unnamed x3, waiting for transfers between devices  18.7 us
    ppermute x6, waiting for transfers between devices, padded(): lax.ppermute(head, axis, [((i + 1) % count, i) for i in range(ends)])  10.8 us
  transfers between devices with their start and end apart: 14, of which 5 were waited for; matrix products, arithmetic and copies ran while one was open for 8% of the time, Pallas kernels for 0%

commit v1 on v0

v1 whole, which is shorter than its diff:
```python
import math

import jax
import jax.numpy as jnp
from jax import lax
from jax.experimental import pallas as pl
from jax.experimental.pallas import tpu as pltpu
from jax.sharding import PartitionSpec as P

MESH = pl.DeviceIdType.MESH
BF, F32 = jnp.bfloat16, jnp.float32
WIN = 128
DH = 32
FEAT = 192
AUG = 208
BLK = AUG + FEAT
PAIRS = 3
GRP = 16
MASKED = -1e30
MARK = 1e4
SCALE = 1.0 / math.sqrt(DH)
EXPC = SCALE * math.log2(math.e)
PARTS = ((0, 1), (1, 3), (3, 4))
NT = (((1,), (1,)), ((), ()))


def dot(a, b):
    return jnp.dot(a, b, preferred_element_type=F32)


def dot_nt(a, b):
    return lax.dot_general(a, b, NT, preferred_element_type=F32)


def iota(shape, dim):
    return lax.broadcasted_iota(jnp.int32, shape, dim)


def diagonal(first, second):
    zero = jnp.zeros_like(first)
    return jnp.concatenate(
        [jnp.concatenate([first, zero], 1), jnp.concatenate([zero, second], 1)], 0
    )


def placed(pair, p, tail):
    pieces = [pair]
    if p > 0:
        pieces = [jnp.zeros((64 * p, 256), BF)] + pieces
    if p < PAIRS - 1:
        pieces = pieces + [jnp.zeros((64 * (PAIRS - 1 - p), 256), BF)]
    return jnp.concatenate(pieces + [tail, jnp.zeros((48, 256), BF)], 0)


def neighbours(w):
    r, c = divmod(w, 2)
    return (
        w - 2 if r else 4 + c,
        6 + c if r else w + 2,
        w - 1 if c else 8 + r,
        10 + r if c else w + 1,
    )


def kernel(
    n_x,
    n_y,
    q_ref,
    k_ref,
    v_ref,
    go_ref,
    ow_ref,
    cnt_ref,
    adj_ref,
    far_ref,
    bo_ref,
    gq_ref,
    gk_ref,
    gv_ref,
    kvx,
    keys,
    kt,
    vt,
    pool,
    gm,
    owt,
    e_s,
    m_s,
    a_s,
    f_s,
    c_s,
    att,
    gq_s,
    g_s,
    pg_out,
    pg_in,
    rim_out,
    rim_in,
    bo_out,
    bo_in,
    bo_own,
    halo_send,
    halo_recv,
    pool_send,
    pool_recv,
    rim_send,
    rim_recv,
    pg_send,
    pg_recv,
    bo_send,
    bo_recv,
):
    sx, sy, hd = lax.axis_index("sx"), lax.axis_index("sy"), lax.axis_index("hd")
    up, down = sx > 0, sx < n_x - 1
    left, right = sy > 0, sy < n_y - 1
    x_lo, x_hi = {"sx": jnp.maximum(sx - 1, 0)}, {"sx": jnp.minimum(sx + 1, n_x - 1)}
    y_lo, y_hi = {"sy": jnp.maximum(sy - 1, 0)}, {"sy": jnp.minimum(sy + 1, n_y - 1)}
    peers = [lax.rem(sy + off, n_y) for off in range(1, n_y)]

    barrier = pltpu.get_barrier_semaphore()

    def greet(where):
        pl.semaphore_signal(barrier, inc=1, device_id=where, device_id_type=MESH)

    pl.when(up)(lambda: greet(x_lo))
    pl.when(down)(lambda: greet(x_hi))
    greet({"hd": 1 - hd})
    for peer in peers:
        greet({"sy": peer})

    pooled = None
    for w in range(4):
        r, c = divmod(w, 2)
        keep = GRP * cnt_ref[r, c]
        off = (iota((16, WIN), 0) == 0) & (iota((16, WIN), 1) >= keep)
        mask = jnp.where(off, MASKED, 0.0).astype(BF)
        block = jnp.concatenate([k_ref[w], mask, v_ref[w]], 0)
        kvx[w] = block
        keys[w, 0] = block
        row, lane = iota((32, WIN), 0), iota((32, WIN), 1)
        member = jnp.where(row == 8 * w + lane // GRP, 1.0, 0.0).astype(BF)
        part = dot_nt(member, jnp.concatenate([k_ref[w], v_ref[w]], 0))
        row, lane = iota((32, 2 * FEAT), 0), iota((32, 2 * FEAT), 1)
        bad = (lane == 0) & (row >= 8 * w + cnt_ref[r, c]) & (row < 8 * w + 8)
        part = jnp.where(bad, MARK, part * (1.0 / GRP))
        pooled = part if pooled is None else pooled + part
    pool[sy] = pooled.astype(BF)

    pl.semaphore_wait(barrier, n_y + up.astype(jnp.int32) + down.astype(jnp.int32))

    def remote(src, dst, sends, recvs, i, j, where):
        return pltpu.make_async_remote_copy(
            src_ref=src,
            dst_ref=dst,
            send_sem=sends.at[i],
            recv_sem=recvs.at[j],
            device_id=where,
            device_id_type=MESH,
        )

    def halo(src, dst, i, where):
        return remote(kvx.at[src], kvx.at[dst], halo_send, halo_recv, i, i, where)

    halos = (
        (up, [halo(pl.ds(0, 2), pl.ds(6, 2), 0, x_lo)]),
        (down, [halo(pl.ds(2, 2), pl.ds(4, 2), 1, x_hi)]),
        (left, [halo(0, 10, 2, y_lo), halo(2, 11, 3, y_lo)]),
        (right, [halo(1, 8, 4, y_hi), halo(3, 9, 5, y_hi)]),
    )
    arrivals = ((up, [1], 4), (down, [0], 6), (left, [4, 5], 8), (right, [2, 3], 10))
    flat = [copy for _, copies in halos for copy in copies]

    def start_all(copies):
        for copy in copies:
            copy.start()

    def wait_sends(copies):
        for copy in copies:
            copy.wait_send()

    def wait_recvs(copies):
        for copy in copies:
            copy.wait_recv()

    pool_copies = [
        remote(pool.at[sy], pool.at[sy], pool_send, pool_recv, i, sy, {"sy": peer})
        for i, peer in enumerate(peers)
    ]
    pool_arrivals = [
        remote(pool.at[peer], pool.at[peer], pool_send, pool_recv, i, peer, {"sy": peer})
        for i, peer in enumerate(peers)
    ]
    for there, copies in halos:
        pl.when(there)(lambda copies=copies: start_all(copies))
    start_all(pool_copies)

    for w in range(4):
        r, c = divmod(w, 2)
        mixed = dot(ow_ref[...], go_ref[w])
        mixed = jnp.where(iota((FEAT, WIN), 1) < GRP * cnt_ref[r, c], mixed, 0.0)
        gm[w] = mixed.astype(BF)
    owt[...] = ow_ref[...].T

    def turn(w, b, block):
        pad = jnp.zeros((48, WIN), BF)
        kt[w, pl.ds(WIN * b, WIN), :] = jnp.concatenate([block[:AUG], pad], 0).T
        vt[w, pl.ds(WIN * b, WIN), :] = jnp.concatenate(
            [block[AUG:], jnp.zeros((64, WIN), BF)], 0
        ).T

    for w in range(4):
        turn(w, 0, keys[w, 0])

    def rows_of(w, part, base, p):
        first, last = PARTS[part]
        return jnp.concatenate(
            [keys[w, b, base + 64 * p : base + 64 * p + 64, :] for b in range(first, last)], 1
        )

    def forward(part):
        first, last = PARTS[part]
        lo, n = WIN * first, WIN * (last - first)
        one_row = jnp.where(iota((16, 256), 0) == 0, 1.0, 0.0).astype(BF)
        ones = jnp.ones((16, n), BF)

        def body(w, carry):
            for p in range(PAIRS):
                pair = diagonal(
                    q_ref[w, 64 * p : 64 * p + 32, :], q_ref[w, 64 * p + 32 : 64 * p + 64, :]
                )
                scores = dot(kt[w, lo : lo + n, :], placed(pair, p, one_row))
                top = jnp.max(scores, axis=0, keepdims=True)
                low = jnp.exp2((scores - top) * EXPC).astype(BF)
                e_s[w, p, lo : lo + n, :] = low
                rows = jnp.concatenate([rows_of(w, part, AUG, p), ones], 0)
                a_s[w, p, part] = dot(rows, low)
                m_s[w, p, part] = jnp.broadcast_to(top, (8, 256))
            return carry

        lax.fori_loop(0, 4, body, 0)

    forward(0)

    for there, index, slot in arrivals:

        def arrive(index=index):
            wait_recvs([flat[i] for i in index])

        def outside(slot=slot):
            off = iota((2, BLK, WIN), 1) == FEAT
            kvx[slot : slot + 2] = jnp.where(off, MASKED, 0.0).astype(BF)

        pl.when(there)(arrive)
        pl.when(jnp.logical_not(there))(outside)

    for w in range(4):
        r, c = divmod(w, 2)
        n0, n1, n2, n3 = neighbours(w)
        for s in range(2):
            code = adj_ref[r, c, s]
            slot = jnp.where(
                code < 2, jnp.where(code == 0, n0, n1), jnp.where(code == 2, n2, n3)
            )
            block = kvx[slot]
            keys[w, 1 + s] = block
            turn(w, 1 + s, block)

    forward(1)

    wait_recvs(pool_arrivals)
    for w in range(4):
        r, c = divmod(w, 2)
        listed = jnp.concatenate([pool[far_ref[r, c, f]] for f in range(4)], 0).T
        bad = (iota((16, WIN), 0) == 0) & (listed[:16].astype(F32) > 0.5 * MARK)
        mask = jnp.where(bad, MASKED, 0.0).astype(BF)
        block = jnp.concatenate([listed[:FEAT], mask, listed[FEAT:]], 0)
        keys[w, 3] = block
        turn(w, 3, block)

    forward(2)

    def combine(w, carry):
        keep = GRP * cnt_ref[w // 2, w % 2]
        for p in range(PAIRS):
            tops = [m_s[w, p, i, 0:1, :] for i in range(3)]
            top = jnp.maximum(jnp.maximum(tops[0], tops[1]), tops[2])
            shares = [jnp.exp2((t - top) * EXPC) for t in tops]
            total = sum(share * a_s[w, p, i] for i, share in enumerate(shares))
            inverse = 1.0 / total[64:65]
            first = total[:32, :WIN] * inverse[:, :WIN]
            second = total[32:64, WIN:] * inverse[:, WIN:]
            both = jnp.concatenate([first, second], 0)
            product = both * gm[w, 64 * p : 64 * p + 64, :].astype(F32)
            centre = jnp.concatenate(
                [
                    jnp.sum(product[:32], axis=0, keepdims=True),
                    jnp.sum(product[32:], axis=0, keepdims=True),
                ],
                1,
            )
            c_s[w, p] = jnp.broadcast_to(centre, (8, 256))
            for i, share in enumerate(shares):
                f_s[w, p, i] = jnp.broadcast_to(share * inverse, (8, 256))
            both = jnp.where(iota((64, WIN), 1) < keep, both, 0.0)
            att[w, 64 * p : 64 * p + 64, :] = both.astype(BF)
        return carry

    lax.fori_loop(0, 4, combine, 0)

    mine = pl.ds(pl.multiple_of(hd * FEAT, FEAT), FEAT)
    theirs = pl.ds(pl.multiple_of((1 - hd) * FEAT, FEAT), FEAT)
    for w in range(4):
        bo_out[w] = dot(owt[theirs, :], att[w]).astype(BF)
    bo_copy = remote(bo_out, bo_in, bo_send, bo_recv, 0, 0, {"hd": 1 - hd})
    bo_copy.start()

    def backward(part):
        first, last = PARTS[part]
        lo, n = WIN * first, WIN * (last - first)
        no_row = jnp.zeros((16, 256), BF)

        def body(w, carry):
            for p in range(PAIRS):
                one, two = slice(64 * p, 64 * p + 32), slice(64 * p + 32, 64 * p + 64)
                factor = f_s[w, p, part, 0:1, :]
                grad_one, grad_two = gm[w, one, :], gm[w, two, :]
                prob = dot(vt[w, lo : lo + n, :], placed(diagonal(grad_one, grad_two), p, no_row))
                low = e_s[w, p, lo : lo + n, :]
                slope = (low.astype(F32) * (prob - c_s[w, p, 0:1, :])).astype(BF)
                scaled = factor * SCALE
                back = dot(rows_of(w, part, 0, p), slope) * scaled
                back = jnp.concatenate([back[:32, :WIN], back[32:, WIN:]], 0)
                if part != 2:
                    back = back + gq_s[w, 64 * p : 64 * p + 64, :]
                if part == 0:
                    gq_ref[w, 64 * p : 64 * p + 64, :] = back.astype(BF)
                else:
                    gq_s[w, 64 * p : 64 * p + 64, :] = back
                rows = diagonal(
                    (q_ref[w, one, :].astype(F32) * scaled[:, :WIN]).astype(BF),
                    (q_ref[w, two, :].astype(F32) * scaled[:, WIN:]).astype(BF),
                )
                g_s[w, 64 * p : 64 * p + 64, lo : lo + n] = dot_nt(rows, slope)
                rows = diagonal(
                    (grad_one.astype(F32) * factor[:, :WIN]).astype(BF),
                    (grad_two.astype(F32) * factor[:, WIN:]).astype(BF),
                )
                g_s[w, FEAT + 64 * p : FEAT + 64 * p + 64, lo : lo + n] = dot_nt(rows, low)
            return carry

        lax.fori_loop(0, 4, body, 0)

    backward(2)

    spread = None
    entries = 32 * n_y
    for w in range(4):
        r, c = divmod(w, 2)
        row, lane = iota((entries, WIN), 0), iota((entries, WIN), 1)
        want = jnp.zeros((entries, WIN), jnp.int32)
        for f in range(4):
            want = jnp.where(lane // 32 == f, 32 * far_ref[r, c, f] + lane - 32 * f, want)
        chosen = jnp.where(row == want, 1.0, 0.0).astype(BF)
        term = dot_nt(chosen, g_s[w, :, 3 * WIN : 4 * WIN].astype(BF))
        spread = term if spread is None else spread + term
    pg_out[...] = spread.astype(BF).reshape(n_y, 32, 2 * FEAT)
    pg_copies = [
        remote(pg_out.at[peer], pg_in.at[sy], pg_send, pg_recv, i, sy, {"sy": peer})
        for i, peer in enumerate(peers)
    ]
    pg_arrivals = [
        remote(pg_out.at[peer], pg_in.at[peer], pg_send, pg_recv, i, peer, {"sy": peer})
        for i, peer in enumerate(peers)
    ]
    start_all(pg_copies)

    backward(1)

    def toward(w, code):
        r, c = divmod(w, 2)
        total = None
        for s in range(2):
            here = (adj_ref[r, c, s] == code).astype(F32)
            term = g_s[w, :, (1 + s) * WIN : (2 + s) * WIN] * here
            total = term if total is None else total + term
        return total

    for w in range(4):
        r, c = divmod(w, 2)
        rim_out[2 * r + c] = toward(w, r).astype(BF)
        rim_out[4 + 2 * c + r] = toward(w, 2 + c).astype(BF)

    def rim(src, dst, i, where):
        return remote(
            rim_out.at[pl.ds(src, 2)], rim_in.at[pl.ds(dst, 2)], rim_send, rim_recv, i, i, where
        )

    rims = ((up, rim(0, 2, 0, x_lo)), (down, rim(2, 0, 1, x_hi)), (left, rim(4, 6, 2, y_lo)), (right, rim(6, 4, 3, y_hi)))
    for there, copy in rims:
        pl.when(there)(copy.start)

    backward(0)

    for w in range(4):
        bo_own[w] = dot(owt[mine, :], att[w])

    bo_copy.wait_recv()
    for w in range(4):
        bo_ref[w] = (bo_own[w] + bo_in[w].astype(F32)).astype(BF)

    for there, i, slot in ((up, 1, 0), (down, 0, 2), (left, 3, 4), (right, 2, 6)):

        def none(slot=slot):
            rim_in[slot : slot + 2] = jnp.zeros((2, 2 * FEAT, WIN), BF)

        pl.when(there)(rims[i][1].wait_recv)
        pl.when(jnp.logical_not(there))(none)

    wait_recvs(pg_arrivals)
    coarse = pg_out[sy].astype(F32)
    for peer in peers:
        coarse = coarse + pg_in[peer].astype(F32)
    coarse = (coarse * (1.0 / GRP)).T.astype(BF)

    for w in range(4):
        r, c = divmod(w, 2)
        total = g_s[w, :, :WIN]
        total = total + toward(w ^ 2, r) + toward(w ^ 1, 2 + c)
        total = total + rim_in[2 * r + c].astype(F32) + rim_in[4 + 2 * c + r].astype(F32)
        member = jnp.where(iota((32, WIN), 0) == 8 * w + iota((32, WIN), 1) // GRP, 1.0, 0.0)
        total = total + dot(coarse, member.astype(BF))
        gk_ref[w] = total[:FEAT].astype(BF)
        gv_ref[w] = total[FEAT:].astype(BF)

    for there, copies in halos:
        pl.when(there)(lambda copies=copies: wait_sends(copies))
    wait_sends(pool_copies)
    wait_sends(pg_copies)
    bo_copy.wait_send()
    for there, copy in rims:
        pl.when(there)(copy.wait_send)


def local(n_x, n_y, queries, key_field, value_field, grad_output, out_weight, counts, adjacent, far_list):
    def flat(x):
        return x.reshape(4, -1, WIN)

    vmem = pl.BlockSpec(memory_space=pltpu.VMEM)
    smem = pl.BlockSpec(memory_space=pltpu.SMEM)
    shape = jax.ShapeDtypeStruct((4, FEAT, WIN), BF)
    dma = pltpu.SemaphoreType.DMA
    outs = pl.pallas_call(
        lambda *refs: kernel(n_x, n_y, *refs),
        out_shape=[shape] * 4,
        in_specs=[vmem] * 5 + [smem] * 3,
        out_specs=[vmem] * 4,
        scratch_shapes=[
            pltpu.VMEM((12, BLK, WIN), BF),
            pltpu.VMEM((4, 4, BLK, WIN), BF),
            pltpu.VMEM((4, 512, 256), BF),
            pltpu.VMEM((4, 512, 256), BF),
            pltpu.VMEM((n_y, 32, 2 * FEAT), BF),
            pltpu.VMEM((4, FEAT, WIN), BF),
            pltpu.VMEM((2 * FEAT, FEAT), BF),
            pltpu.VMEM((4, PAIRS, 512, 256), BF),
            pltpu.VMEM((4, PAIRS, 3, 8, 256), F32),
            pltpu.VMEM((4, PAIRS, 3, 80, 256), F32),
            pltpu.VMEM((4, PAIRS, 3, 8, 256), F32),
            pltpu.VMEM((4, PAIRS, 8, 256), F32),
            pltpu.VMEM((4, FEAT, WIN), BF),
            pltpu.VMEM((4, FEAT, WIN), F32),
            pltpu.VMEM((4, 2 * FEAT, 512), F32),
            pltpu.VMEM((n_y, 32, 2 * FEAT), BF),
            pltpu.VMEM((n_y, 32, 2 * FEAT), BF),
            pltpu.VMEM((8, 2 * FEAT, WIN), BF),
            pltpu.VMEM((8, 2 * FEAT, WIN), BF),
            pltpu.VMEM((4, FEAT, WIN), BF),
            pltpu.VMEM((4, FEAT, WIN), BF),
            pltpu.VMEM((4, FEAT, WIN), F32),
            dma((6,)),
            dma((6,)),
            dma((n_y,)),
            dma((n_y,)),
            dma((4,)),
            dma((4,)),
            dma((n_y,)),
            dma((n_y,)),
            dma((1,)),
            dma((1,)),
        ],
        compiler_params=pltpu.CompilerParams(
            collective_id=0, has_side_effects=True, vmem_limit_bytes=48 * 1024 * 1024
        ),
    )(flat(queries), flat(key_field), flat(value_field), flat(grad_output), out_weight, counts, adjacent, far_list)
    block_out, grad_queries, grad_keys, grad_values = outs
    return (
        block_out.reshape(2, 2, FEAT, WIN),
        grad_queries.reshape(queries.shape),
        grad_keys.reshape(queries.shape),
        grad_values.reshape(queries.shape),
    )


def solution(mesh):
    n_x, n_y = mesh.shape["sx"], mesh.shape["sy"]
    grid = P("sx", "sy")
    heads = P("sx", "sy", "hd", None, None)
    return jax.shard_map(
        lambda *args: local(n_x, n_y, *args),
        mesh=mesh,
        in_specs=(heads, heads, heads, grid, P("hd", None), grid, grid, grid),
        out_specs=(P("sx", "sy", "hd", None), heads, heads, heads),
        check_vma=False,
    )
```

time: 334 us -> 51.2 us (0.15)
  matrix products: 67.2 us -> 0 us
  other arithmetic: 62.2 us -> 0 us
  waiting for transfers between devices: 49.7 us -> 0 us
  local copies, waits for them, and re-layouts: 57.2 us -> 8.08 us
  Pallas kernels: 0 us -> 42.2 us
  blocking collectives: 42 us -> 0 us
  starting transfers between devices: 32.9 us -> 0 us
  between operations: 16.6 us -> 0.67 us
    dot_general x14 -> x0, matrix products: 67.2 us -> none  [the longest x2 25.7 us: window_pass(): jnp.einsum('bhij,bhdi->bhdj', grad_score, query_rows, preferred_element_t...]
    pallas_call x0 -> x1, Pallas kernels: none -> 42.2 us  [local(): pl.pallas_call(lambda *refs: kernel(n_x, n_y, *refs), out_shape=[shape] *...]
    all_gather x2 -> x0, blocking collectives: 42 us -> none  [the longest x1 21.2 us: local(): lax.all_gather(pooled_mask, 'sy', axis=1, tiled=True)]
    ppermute x12 -> x0, starting transfers between devices: 32.8 us -> none  [the longest x6 23 us: padded(): lax.ppermute(tail, axis, [(i, (i + 1) % count) for i in range(ends)])]
    scatter-add x10 -> x0, other arithmetic: 26.4 us -> none  [the longest x2 7.86 us: row_step(): strip_grads = strip_grads.at[far_row].add(far_grad)]
    reduce_scatter x1 -> x0, waiting for transfers between devices: 19.4 us -> none  [local(): lax.psum_scatter(strip_grads.astype(jnp.bfloat16), 'sy', scatter_dimensio...]
    unnamed x3 -> x0, waiting for transfers between devices: 18.7 us -> none
    gather x12 -> x0, local copies, waits for them, and re-layouts: 14 us -> none  [the longest x4 5.44 us: row_step(): far_part = strip_kv[far_row]]
  transfers between devices with their start and end apart: 14 -> 0, of which waited for: 5 -> 0; matrix products, arithmetic and copies ran while one was open for 8% -> 0% of each run, Pallas kernels for 0% -> 0%
where the time goes in v1:
time: 51.2 us; the launch traced here: 50.9 us
  Pallas kernels  42.2 us (82%)
  local copies, waits for them, and re-layouts  8.08 us (16%)
  between operations  0.67 us (1%)
    pallas_call x1, Pallas kernels, local(): pl.pallas_call(lambda *refs: kernel(n_x, n_y, *refs), out_shape=[shape] *...  42.2 us
    unnamed x20, local copies, waits for them, and re-layouts  8.08 us

profile of v1, /device:TPU:1, one launch (start us, length us, event | category | flops | bytes accessed | tf_op | source)
XLA Modules:
  0.0 50.9 jit_solution(7607753460918496427)
XLA Ops:
  0.6 0.0 copy-start.6
  0.6 0.0 copy-start.5
  0.7 0.0 copy-start.7
  0.7 0.7 %copy-done.6 = s32[2,2,4]{2,1,0:T(2,128)S(1)} copy-done((s32[2,2,4]{2,1,0:T(2,128)S(1)}, s32[2,2,4]{2,1,0:T(2,128)}, u32[]{:S(2)}) %copy-start.6) | copy-done | bytes 88
  1.3 0.0 copy-done.5
  1.3 0.0 copy-done.7
  1.3 0.0 copy-start
  1.3 1.0 %copy-done = bf16[2,2,384,128]{3,2,1,0:T(8,128)(2,1)S(1)} copy-done((bf16[2,2,384,128]{3,2,1,0:T(8,128)(2,1)S(1)}, bf16[2,2,384,128]{3,2,1,0:T(8,128)(2,1)}, u32[]{:S(2)}) %copy-start) | copy-done | bytes 393240
  2.3 0.0 copy-start.1
  2.3 0.9 %copy-done.1 = bf16[2,2,6,32,128]{4,3,2,1,0:T(8,128)(2,1)S(1)} copy-done((bf16[2,2,6,32,128]{4,3,2,1,0:T(8,128)(2,1)S(1)}, bf16[2,2,6,32,128]{4,3,2,1,0:T(8,128)(2,1)}, u32[]{:S(2)}) %copy-start.1) | copy-done | bytes 196632
  3.3 0.0 copy-start.2
  3.3 0.9 %copy-done.2 = bf16[2,2,6,32,128]{4,3,2,1,0:T(8,128)(2,1)S(1)} copy-done((bf16[2,2,6,32,128]{4,3,2,1,0:T(8,128)(2,1)S(1)}, bf16[2,2,6,32,128]{4,3,2,1,0:T(8,128)(2,1)}, u32[]{:S(2)}) %copy-start.2) | copy-done | bytes 196632
  4.2 0.0 copy-start.3
  4.2 0.9 %copy-done.3 = bf16[2,2,6,32,128]{4,3,2,1,0:T(8,128)(2,1)S(1)} copy-done((bf16[2,2,6,32,128]{4,3,2,1,0:T(8,128)(2,1)S(1)}, bf16[2,2,6,32,128]{4,3,2,1,0:T(8,128)(2,1)}, u32[]{:S(2)}) %copy-start.3) | copy-done | bytes 196632
  5.1 0.0 copy-start.4
  5.1 0.9 %copy-done.4 = bf16[192,384]{1,0:T(8,128)(2,1)S(1)} copy-done((bf16[192,384]{1,0:T(8,128)(2,1)S(1)}, bf16[192,384]{1,0:T(8,128)(2,1)}, u32[]{:S(2)}) %copy-start.4) | copy-done | bytes 147480
  6.0 42.2 %shard_map.111 = (bf16[4,192,128]{2,1,0:T(8,128)(2,1)S(1)}, bf16[4,192,128]{2,1,0:T(8,128)(2,1)S(1)}, bf16[4,192,128]{2,1,0:T(8,128)(2,1)S(1)}, bf16[4,192,128]{2,1,0:T(8,128)(2,1)S(1)}) custom-call(bf16[4,192,128]{2,1,0:T(8,128)(2,1)S(1)} %bitcast.13, bf16[4,192,128]{2,1,0:T(8,128)(2,1)S(1)} %bitcast.14, bf16[4,192,128]{2,1,0:T(8,128)(2,1)S(1)} %bitcast.15, ...), custom_call_target="tpu_custom_call" | custom-call | tf_op jit(solution)/shard_map/pallas_call | solution.py:452
  48.2 0.7 %copy.16 = bf16[2,2,192,128]{3,2,1,0:T(8,128)(2,1)} copy(bf16[2,2,192,128]{3,2,1,0:T(8,128)(2,1)S(1)} %bitcast.12) | data formatting | bytes 393216
  48.9 0.7 %copy.17 = bf16[2,2,6,32,128]{4,3,2,1,0:T(8,128)(2,1)} copy(bf16[2,2,6,32,128]{4,3,2,1,0:T(8,128)(2,1)S(1)} %bitcast.11) | data formatting | bytes 393216
  49.6 0.7 %copy.18 = bf16[2,2,6,32,128]{4,3,2,1,0:T(8,128)(2,1)} copy(bf16[2,2,6,32,128]{4,3,2,1,0:T(8,128)(2,1)S(1)} %bitcast.10) | data formatting | bytes 393216
  50.2 0.7 %copy.19 = bf16[2,2,6,32,128]{4,3,2,1,0:T(8,128)(2,1)} copy(bf16[2,2,6,32,128]{4,3,2,1,0:T(8,128)(2,1)S(1)} %bitcast.9) | data formatting | bytes 393216
Async XLA Ops:
  0.6 0.7 %copy-start.6 = (s32[2,2,4]{2,1,0:T(2,128)S(1)}, s32[2,2,4]{2,1,0:T(2,128)}, u32[]{:S(2)}) copy-start(s32[2,2,4]{2,1,0:T(2,128)} %refs_7_.1) | copy-start | bytes 196
  0.6 0.7 %copy-start.5 = (s32[2,2,2]{2,1,0:T(2,128)S(1)}, s32[2,2,2]{2,1,0:T(2,128)}, u32[]{:S(2)}) copy-start(s32[2,2,2]{2,1,0:T(2,128)} %refs_6_.1) | copy-start | bytes 100
  0.7 0.7 %copy-start.7 = (s32[2,2]{1,0:T(2,128)S(1)}, s32[2,2]{1,0:T(2,128)}, u32[]{:S(2)}) copy-start(s32[2,2]{1,0:T(2,128)} %refs_5_.1) | copy-start | bytes 52
  1.3 1.0 %copy-start = (bf16[2,2,384,128]{3,2,1,0:T(8,128)(2,1)S(1)}, bf16[2,2,384,128]{3,2,1,0:T(8,128)(2,1)}, u32[]{:S(2)}) copy-start(bf16[2,2,384,128]{3,2,1,0:T(8,128)(2,1)} %param.11) | copy-start | bytes 1179652
  2.3 0.9 %copy-start.1 = (bf16[2,2,6,32,128]{4,3,2,1,0:T(8,128)(2,1)S(1)}, bf16[2,2,6,32,128]{4,3,2,1,0:T(8,128)(2,1)}, u32[]{:S(2)}) copy-start(bf16[2,2,6,32,128]{4,3,2,1,0:T(8,128)(2,1)} %param.8) | copy-start | bytes 589828
  3.3 0.9 %copy-start.2 = (bf16[2,2,6,32,128]{4,3,2,1,0:T(8,128)(2,1)S(1)}, bf16[2,2,6,32,128]{4,3,2,1,0:T(8,128)(2,1)}, u32[]{:S(2)}) copy-start(bf16[2,2,6,32,128]{4,3,2,1,0:T(8,128)(2,1)} %param.9) | copy-start | bytes 589828
  4.2 0.9 %copy-start.3 = (bf16[2,2,6,32,128]{4,3,2,1,0:T(8,128)(2,1)S(1)}, bf16[2,2,6,32,128]{4,3,2,1,0:T(8,128)(2,1)}, u32[]{:S(2)}) copy-start(bf16[2,2,6,32,128]{4,3,2,1,0:T(8,128)(2,1)} %param.10) | copy-start | bytes 589828
  5.1 0.9 %copy-start.4 = (bf16[192,384]{1,0:T(8,128)(2,1)S(1)}, bf16[192,384]{1,0:T(8,128)(2,1)}, u32[]{:S(2)}) copy-start(bf16[192,384]{1,0:T(8,128)(2,1)} %refs_4_.1) | copy-start | bytes 442372

commit v2 on v1

--- a/solution.py
+++ b/solution.py
@@ -16,6 +16,7 @@
 BLK = AUG + FEAT
 PAIRS = 3
 GRP = 16
+VMEM = 63 * 1024 * 1024
 MASKED = -1e30
 MARK = 1e4
 SCALE = 1.0 / math.sqrt(DH)
@@ -65,14 +66,24 @@
 def kernel(
     n_x,
     n_y,
-    q_ref,
-    k_ref,
-    v_ref,
-    go_ref,
-    ow_ref,
+    q_in,
+    k_in,
+    v_in,
+    go_in,
+    ow_in,
+    cnt_in,
+    adj_in,
+    far_in,
+    bo_out_ref,
+    gq_out_ref,
+    gk_out_ref,
+    gv_out_ref,
     cnt_ref,
     adj_ref,
     far_ref,
+    q_ref,
+    go_ref,
+    ow_ref,
     bo_ref,
     gq_ref,
     gk_ref,
@@ -109,6 +120,8 @@
     pg_recv,
     bo_send,
     bo_recv,
+    in_sem,
+    out_sem,
 ):
     sx, sy, hd = lax.axis_index("sx"), lax.axis_index("sy"), lax.axis_index("hd")
     up, down = sx > 0, sx < n_x - 1
@@ -128,18 +141,39 @@
     for peer in peers:
         greet({"sy": peer})
 
+    reads = [
+        pltpu.make_async_copy(src, dst, in_sem.at[i])
+        for i, (src, dst) in enumerate(
+            (
+                (k_in, kvx.at[pl.ds(0, 4), pl.ds(0, FEAT)]),
+                (v_in, kvx.at[pl.ds(0, 4), pl.ds(AUG, FEAT)]),
+                (go_in, go_ref),
+                (ow_in, ow_ref),
+                (q_in, q_ref),
+                (adj_in, adj_ref),
+                (far_in, far_ref),
+                (cnt_in, cnt_ref),
+            )
+        )
+    ]
+    for copy in reads:
+        copy.start()
+
+    reads[0].wait()
+    reads[1].wait()
+    reads[7].wait()
     pooled = None
     for w in range(4):
         r, c = divmod(w, 2)
         keep = GRP * cnt_ref[r, c]
         off = (iota((16, WIN), 0) == 0) & (iota((16, WIN), 1) >= keep)
         mask = jnp.where(off, MASKED, 0.0).astype(BF)
-        block = jnp.concatenate([k_ref[w], mask, v_ref[w]], 0)
-        kvx[w] = block
+        kvx[w, FEAT:AUG] = mask
+        block = kvx[w]
         keys[w, 0] = block
         row, lane = iota((32, WIN), 0), iota((32, WIN), 1)
         member = jnp.where(row == 8 * w + lane // GRP, 1.0, 0.0).astype(BF)
-        part = dot_nt(member, jnp.concatenate([k_ref[w], v_ref[w]], 0))
+        part = dot_nt(member, jnp.concatenate([block[:FEAT], block[AUG:]], 0))
         row, lane = iota((32, 2 * FEAT), 0), iota((32, 2 * FEAT), 1)
         bad = (lane == 0) & (row >= 8 * w + cnt_ref[r, c]) & (row < 8 * w + 8)
         part = jnp.where(bad, MARK, part * (1.0 / GRP))
@@ -194,6 +228,8 @@
         pl.when(there)(lambda copies=copies: start_all(copies))
     start_all(pool_copies)
 
+    for copy in reads[2:7]:
+        copy.wait()
     for w in range(4):
         r, c = divmod(w, 2)
         mixed = dot(ow_ref[...], go_ref[w])
@@ -224,20 +260,25 @@
         ones = jnp.ones((16, n), BF)
 
         def body(w, carry):
+            scores, tops, lows, sums = [], [], [], []
             for p in range(PAIRS):
                 pair = diagonal(
                     q_ref[w, 64 * p : 64 * p + 32, :], q_ref[w, 64 * p + 32 : 64 * p + 64, :]
                 )
-                scores = dot(kt[w, lo : lo + n, :], placed(pair, p, one_row))
-                top = jnp.max(scores, axis=0, keepdims=True)
-                low = jnp.exp2((scores - top) * EXPC).astype(BF)
-                e_s[w, p, lo : lo + n, :] = low
-                rows = jnp.concatenate([rows_of(w, part, AUG, p), ones], 0)
-                a_s[w, p, part] = dot(rows, low)
-                m_s[w, p, part] = jnp.broadcast_to(top, (8, 256))
+                scores.append(dot(kt[w, lo : lo + n, :], placed(pair, p, one_row)))
+            rows = [jnp.concatenate([rows_of(w, part, AUG, p), ones], 0) for p in range(PAIRS)]
+            for p in range(PAIRS):
+                tops.append(jnp.max(scores[p], axis=0, keepdims=True))
+                lows.append(jnp.exp2((scores[p] - tops[p]) * EXPC).astype(BF))
+            for p in range(PAIRS):
+                sums.append(dot(rows[p], lows[p]))
+            for p in range(PAIRS):
+                e_s[w, p, lo : lo + n, :] = lows[p]
+                a_s[w, p, part] = sums[p]
+                m_s[w, p, part] = jnp.broadcast_to(tops[p], (8, 256))
             return carry
 
-        lax.fori_loop(0, 4, body, 0)
+        lax.fori_loop(0, 4, body, 0, unroll=4)
 
     forward(0)
 
@@ -320,35 +361,46 @@
         no_row = jnp.zeros((16, 256), BF)
 
         def body(w, carry):
+            factors = [f_s[w, p, part, 0:1, :] for p in range(PAIRS)]
+            lows = [e_s[w, p, lo : lo + n, :] for p in range(PAIRS)]
+            olds = [gq_s[w, 64 * p : 64 * p + 64, :] for p in range(PAIRS)]
+            slopes, backs, key_terms, value_terms = [], [], [], []
+            heads = [
+                (q_ref[w, 32 * h : 32 * h + 32, :], gm[w, 32 * h : 32 * h + 32, :])
+                for h in range(2 * PAIRS)
+            ]
+            keyrows = [rows_of(w, part, 0, p) for p in range(PAIRS)]
             for p in range(PAIRS):
-                one, two = slice(64 * p, 64 * p + 32), slice(64 * p + 32, 64 * p + 64)
-                factor = f_s[w, p, part, 0:1, :]
-                grad_one, grad_two = gm[w, one, :], gm[w, two, :]
-                prob = dot(vt[w, lo : lo + n, :], placed(diagonal(grad_one, grad_two), p, no_row))
-                low = e_s[w, p, lo : lo + n, :]
-                slope = (low.astype(F32) * (prob - c_s[w, p, 0:1, :])).astype(BF)
-                scaled = factor * SCALE
-                back = dot(rows_of(w, part, 0, p), slope) * scaled
-                back = jnp.concatenate([back[:32, :WIN], back[32:, WIN:]], 0)
-                if part != 2:
-                    back = back + gq_s[w, 64 * p : 64 * p + 64, :]
+                pair = diagonal(heads[2 * p][1], heads[2 * p + 1][1])
+                prob = dot(vt[w, lo : lo + n, :], placed(pair, p, no_row))
+                slopes.append((lows[p].astype(F32) * (prob - c_s[w, p, 0:1, :])).astype(BF))
+            for p in range(PAIRS):
+                scaled = factors[p] * SCALE
+                (q_one, grad_one), (q_two, grad_two) = heads[2 * p], heads[2 * p + 1]
+                back = dot(keyrows[p], slopes[p]) * scaled
+                backs.append(jnp.concatenate([back[:32, :WIN], back[32:, WIN:]], 0))
+                rows = diagonal(
+                    (q_one.astype(F32) * scaled[:, :WIN]).astype(BF),
+                    (q_two.astype(F32) * scaled[:, WIN:]).astype(BF),
+                )
+                key_terms.append(dot_nt(rows, slopes[p]))
+                rows = diagonal(
+                    (grad_one.astype(F32) * factors[p][:, :WIN]).astype(BF),
+                    (grad_two.astype(F32) * factors[p][:, WIN:]).astype(BF),
+                )
+                value_terms.append(dot_nt(rows, lows[p]))
+            for p in range(PAIRS):
+                at = slice(64 * p, 64 * p + 64)
+                back = backs[p] if part == 2 else backs[p] + olds[p]
                 if part == 0:
-                    gq_ref[w, 64 * p : 64 * p + 64, :] = back.astype(BF)
+                    gq_ref[w, at, :] = back.astype(BF)
                 else:
-                    gq_s[w, 64 * p : 64 * p + 64, :] = back
-                rows = diagonal(
-                    (q_ref[w, one, :].astype(F32) * scaled[:, :WIN]).astype(BF),
-                    (q_ref[w, two, :].astype(F32) * scaled[:, WIN:]).astype(BF),
-                )
-                g_s[w, 64 * p : 64 * p + 64, lo : lo + n] = dot_nt(rows, slope)
-                rows = diagonal(
-                    (grad_one.astype(F32) * factor[:, :WIN]).astype(BF),
-                    (grad_two.astype(F32) * factor[:, WIN:]).astype(BF),
-                )
-                g_s[w, FEAT + 64 * p : FEAT + 64 * p + 64, lo : lo + n] = dot_nt(rows, low)
+                    gq_s[w, at, :] = back
+                g_s[w, at, lo : lo + n] = key_terms[p]
+                g_s[w, FEAT + 64 * p : FEAT + 64 * p + 64, lo : lo + n] = value_terms[p]
             return carry
 
-        lax.fori_loop(0, 4, body, 0)
+        lax.fori_loop(0, 4, body, 0, unroll=4)
 
     backward(2)
 
@@ -404,9 +456,18 @@
     for w in range(4):
         bo_own[w] = dot(owt[mine, :], att[w])
 
+    writes = [
+        pltpu.make_async_copy(src, dst, out_sem.at[i])
+        for i, (src, dst) in enumerate(
+            ((gq_ref, gq_out_ref), (bo_ref, bo_out_ref), (gk_ref, gk_out_ref), (gv_ref, gv_out_ref))
+        )
+    ]
+    writes[0].start()
+
     bo_copy.wait_recv()
     for w in range(4):
         bo_ref[w] = (bo_own[w] + bo_in[w].astype(F32)).astype(BF)
+    writes[1].start()
 
     for there, i, slot in ((up, 1, 0), (down, 0, 2), (left, 3, 4), (right, 2, 6)):
 
@@ -431,6 +492,8 @@
         total = total + dot(coarse, member.astype(BF))
         gk_ref[w] = total[:FEAT].astype(BF)
         gv_ref[w] = total[FEAT:].astype(BF)
+    writes[2].start()
+    writes[3].start()
 
     for there, copies in halos:
         pl.when(there)(lambda copies=copies: wait_sends(copies))
@@ -439,6 +502,18 @@
     bo_copy.wait_send()
     for there, copy in rims:
         pl.when(there)(copy.wait_send)
+    for copy in writes:
+        copy.wait()
+
+
+def hand_over(*refs):
+    copies = [
+        pltpu.make_async_copy(refs[i], refs[4 + i], refs[8].at[i]) for i in range(4)
+    ]
+    for copy in copies:
+        copy.start()
+    for copy in copies:
+        copy.wait()
 
 
 def local(n_x, n_y, queries, key_field, value_field, grad_output, out_weight, counts, adjacent, far_list):
@@ -446,15 +521,25 @@
         return x.reshape(4, -1, WIN)
 
     vmem = pl.BlockSpec(memory_space=pltpu.VMEM)
-    smem = pl.BlockSpec(memory_space=pltpu.SMEM)
+    hbm = pl.BlockSpec(memory_space=pl.ANY)
     shape = jax.ShapeDtypeStruct((4, FEAT, WIN), BF)
     dma = pltpu.SemaphoreType.DMA
     outs = pl.pallas_call(
         lambda *refs: kernel(n_x, n_y, *refs),
         out_shape=[shape] * 4,
-        in_specs=[vmem] * 5 + [smem] * 3,
-        out_specs=[vmem] * 4,
+        in_specs=[hbm] * 8,
+        out_specs=[hbm] * 4,
         scratch_shapes=[
+            pltpu.SMEM(counts.shape, jnp.int32),
+            pltpu.SMEM(adjacent.shape, jnp.int32),
+            pltpu.SMEM(far_list.shape, jnp.int32),
+            pltpu.VMEM((4, FEAT, WIN), BF),
+            pltpu.VMEM((4, 2 * FEAT, WIN), BF),
+            pltpu.VMEM((FEAT, 2 * FEAT), BF),
+            pltpu.VMEM((4, FEAT, WIN), BF),
+            pltpu.VMEM((4, FEAT, WIN), BF),
+            pltpu.VMEM((4, FEAT, WIN), BF),
+            pltpu.VMEM((4, FEAT, WIN), BF),
             pltpu.VMEM((12, BLK, WIN), BF),
             pltpu.VMEM((4, 4, BLK, WIN), BF),
             pltpu.VMEM((4, 512, 256), BF),
@@ -487,12 +572,21 @@
             dma((n_y,)),
             dma((1,)),
             dma((1,)),
+            dma((8,)),
+            dma((4,)),
         ],
         compiler_params=pltpu.CompilerParams(
-            collective_id=0, has_side_effects=True, vmem_limit_bytes=48 * 1024 * 1024
+            collective_id=0, has_side_effects=True, vmem_limit_bytes=VMEM
         ),
     )(flat(queries), flat(key_field), flat(value_field), flat(grad_output), out_weight, counts, adjacent, far_list)
-    block_out, grad_queries, grad_keys, grad_values = outs
+    block_out, grad_queries, grad_keys, grad_values = pl.pallas_call(
+        hand_over,
+        out_shape=[shape] * 4,
+        in_specs=[vmem] * 4,
+        out_specs=[hbm] * 4,
+        scratch_shapes=[dma((4,))],
+        compiler_params=pltpu.CompilerParams(vmem_limit_bytes=VMEM),
+    )(*outs)
     return (
         block_out.reshape(2, 2, FEAT, WIN),
         grad_queries.reshape(queries.shape),

time: 51.2 us -> 42.2 us (0.82)
  local copies, waits for them, and re-layouts: 8.08 us -> 0 us
  Pallas kernels: 42.2 us -> 41.4 us
    unnamed x20 -> x0, local copies, waits for them, and re-layouts: 8.08 us -> none
    pallas_call x1, Pallas kernels: 42.2 us -> 39.3 us  [local(): pl.pallas_call(lambda *refs: kernel(n_x, n_y, *refs), out_shape=[shape] *...]
    pallas_call x0 -> x1, Pallas kernels: none -> 2.12 us  [local(): pl.pallas_call(hand_over, out_shape=[shape] * 4, in_specs=[vmem] * 4, out...]
where the time goes in v2:
time: 42.2 us; the launch traced here: 42.1 us
  Pallas kernels  41.4 us (98%)
  between operations  0.64 us (2%)
    pallas_call x1, Pallas kernels, local(): pl.pallas_call(lambda *refs: kernel(n_x, n_y, *refs), out_shape=[shape] *...  39.3 us
    pallas_call x1, Pallas kernels, local(): pl.pallas_call(hand_over, out_shape=[shape] * 4, in_specs=[vmem] * 4, out...  2.12 us

profile of v2, /device:TPU:1, one launch (start us, length us, event | category | flops | bytes accessed | tf_op | source)
XLA Modules:
  0.0 42.1 jit_solution(11866589951732877117)
XLA Ops:
  0.6 39.3 %shard_map.111 = (bf16[4,192,128]{2,1,0:T(8,128)(2,1)}, bf16[4,192,128]{2,1,0:T(8,128)(2,1)}, bf16[4,192,128]{2,1,0:T(8,128)(2,1)}, bf16[4,192,128]{2,1,0:T(8,128)(2,1)}) custom-call(bf16[4,192,128]{2,1,0:T(8,128)(2,1)} %bitcast.9, bf16[4,192,128]{2,1,0:T(8,128)(2,1)} %bitcast.10, bf16[4,192,128]{2,1,0:T(8,128)(2,1)} %bitcast.11, ...), custom_call_target="tpu_custom_call" | custom-call | tf_op jit(solution)/shard_map/pallas_call | solution.py:527
  39.9 2.1 %shard_map.112 = (bf16[4,192,128]{2,1,0:T(8,128)(2,1)}, bf16[4,192,128]{2,1,0:T(8,128)(2,1)}, bf16[4,192,128]{2,1,0:T(8,128)(2,1)}, bf16[4,192,128]{2,1,0:T(8,128)(2,1)}) custom-call(bf16[4,192,128]{2,1,0:T(8,128)(2,1)} %get-tuple-element.12.refs_0_, bf16[4,192,128]{2,1,0:T(8,128)(2,1)} %get-tuple-element.13.refs_1_, ...), custom_call_target="tpu_custom_call" | custom-call | tf_op jit(solution)/shard_map/pallas_call | solution.py:582

commit v3 on v2

v3 whole, which is shorter than its diff:
```python
import math

import jax
import jax.numpy as jnp
from jax import lax
from jax.experimental import pallas as pl
from jax.experimental.pallas import tpu as pltpu
from jax.sharding import PartitionSpec as P

MESH = pl.DeviceIdType.MESH
BF, F32 = jnp.bfloat16, jnp.float32
WIN = 128
DH = 32
FEAT = 192
AUG = 208
PAIRS = 3
GRP = 16
VMEM = 63 * 1024 * 1024
MASKED = -1e30
MARK = 1e4
SCALE = 1.0 / math.sqrt(DH)
EXPC = SCALE * math.log2(math.e)
PARTS = ((0, 1), (1, 3), (3, 4))
NT = (((1,), (1,)), ((), ()))


def dot(a, b):
    return jnp.dot(a, b, preferred_element_type=F32)


def dot_nt(a, b):
    return lax.dot_general(a, b, NT, preferred_element_type=F32)


def iota(shape, dim):
    return lax.broadcasted_iota(jnp.int32, shape, dim)


def diagonal(first, second):
    zero = jnp.zeros_like(first)
    return jnp.concatenate(
        [jnp.concatenate([first, zero], 1), jnp.concatenate([zero, second], 1)], 0
    )


def placed(pair, p, tail):
    pieces = [pair]
    if p > 0:
        pieces = [jnp.zeros((64 * p, 256), BF)] + pieces
    if p < PAIRS - 1:
        pieces = pieces + [jnp.zeros((64 * (PAIRS - 1 - p), 256), BF)]
    return jnp.concatenate(pieces + [tail, jnp.zeros((48, 256), BF)], 0)


def neighbours(w):
    r, c = divmod(w, 2)
    return (
        w - 2 if r else 4 + c,
        6 + c if r else w + 2,
        w - 1 if c else 8 + r,
        10 + r if c else w + 1,
    )


def pack(x):
    tail = jnp.concatenate([x[:, :16, WIN:], x[:, 16:, WIN:]], 2)
    return jnp.concatenate([x[:, :, :WIN], tail], 1)


def unpack(x):
    tail = jnp.concatenate([x[32:, :64], x[32:, 64:]], 0)
    return jnp.concatenate([x[:32], tail], 1)


def kernel(
    n_x,
    n_y,
    q_in,
    k_in,
    v_in,
    go_in,
    ow_in,
    cnt_in,
    adj_in,
    far_in,
    bo_out_ref,
    gq_out_ref,
    gk_out_ref,
    gv_out_ref,
    cnt_ref,
    adj_ref,
    far_ref,
    q_ref,
    go_ref,
    ow_ref,
    bo_ref,
    gq_ref,
    gk_ref,
    gv_ref,
    kx,
    vx,
    kk,
    vv,
    kt,
    vt,
    pool_k,
    pool_v,
    gm,
    owt,
    e_s,
    m_s,
    a_s,
    f_s,
    c_s,
    att,
    gq_s,
    g_s,
    pg_out,
    pg_half,
    pg_sum,
    pg_in,
    rim_out,
    rim_in,
    bo_out,
    bo_in,
    bo_own,
    halo_send,
    halo_recv,
    pool_send,
    pool_recv,
    rim_send,
    rim_recv,
    pg_send,
    pg_recv,
    half_send,
    half_recv,
    bo_send,
    bo_recv,
    in_sem,
    out_sem,
):
    sx, sy, hd = lax.axis_index("sx"), lax.axis_index("sy"), lax.axis_index("hd")
    up, down = sx > 0, sx < n_x - 1
    left, right = sy > 0, sy < n_y - 1
    x_lo, x_hi = {"sx": jnp.maximum(sx - 1, 0)}, {"sx": jnp.minimum(sx + 1, n_x - 1)}
    y_lo, y_hi = {"sy": jnp.maximum(sy - 1, 0)}, {"sy": jnp.minimum(sy + 1, n_y - 1)}
    n_z = n_y // 2
    z, core = sy // 2, lax.rem(sy, 2)
    sibling = {"sy": sy + 1 - 2 * core}
    outer = {"sy": lax.rem(sy + 2 * core - 1 + n_y, n_y)}
    partner = {"hd": 1 - hd}

    def chip_at(step):
        return lax.rem(z + step + n_z, n_z)

    barrier = pltpu.get_barrier_semaphore()

    def greet(where):
        pl.semaphore_signal(barrier, inc=1, device_id=where, device_id_type=MESH)

    steps = sorted(range(1, n_z), key=lambda step: -min(step, n_z - step))
    others = [chip_at(step) for step in steps]
    for chip in others:
        greet({"sy": 2 * chip + core})
    pl.when(up)(lambda: greet(x_lo))
    pl.when(down)(lambda: greet(x_hi))
    for where in (partner, outer, sibling):
        greet(where)

    reads = [
        pltpu.make_async_copy(src, dst, in_sem.at[i])
        for i, (src, dst) in enumerate(
            (
                (k_in, kx.at[pl.ds(0, 4), pl.ds(0, FEAT)]),
                (v_in, vx.at[pl.ds(0, 4)]),
                (cnt_in, cnt_ref),
                (go_in, go_ref),
                (ow_in, ow_ref),
                (q_in, q_ref),
                (adj_in, adj_ref),
                (far_in, far_ref),
            )
        )
    ]
    for copy in reads:
        copy.start()

    for copy in reads[:3]:
        copy.wait()
    pooled_k = pooled_v = None
    for w in range(4):
        r, c = divmod(w, 2)
        keep = GRP * cnt_ref[r, c]
        off = (iota((16, WIN), 0) == 0) & (iota((16, WIN), 1) >= keep)
        kx[w, FEAT:AUG] = jnp.where(off, MASKED, 0.0).astype(BF)
        row, lane = iota((32, WIN), 0), iota((32, WIN), 1)
        member = jnp.where(row == 8 * w + lane // GRP, 1.0, 0.0).astype(BF)
        row, lane = iota((32, FEAT), 0), iota((32, FEAT), 1)
        bad = (lane == 0) & (row >= 8 * w + cnt_ref[r, c]) & (row < 8 * w + 8)
        part = dot_nt(member, kx[w, 0:FEAT]) * (1.0 / GRP)
        part = jnp.where(bad, MARK, part)
        pooled_k = part if pooled_k is None else pooled_k + part
        part = dot_nt(member, vx[w]) * (1.0 / GRP)
        pooled_v = part if pooled_v is None else pooled_v + part
    pool_k[z, core] = pack(pooled_k[None])[0].astype(BF)
    pool_v[z, core] = pack(pooled_v[None])[0].astype(BF)

    pl.semaphore_wait(barrier, n_z + 2 + up.astype(jnp.int32) + down.astype(jnp.int32))

    def remote(src, dst, sends, recvs, i, j, where):
        return pltpu.make_async_remote_copy(
            src_ref=src,
            dst_ref=dst,
            send_sem=sends.at[i],
            recv_sem=recvs.at[j],
            device_id=where,
            device_id_type=MESH,
        )

    def start_all(copies):
        for copy in copies:
            copy.start()

    def wait_sends(copies):
        for copy in copies:
            copy.wait_send()

    def wait_recvs(copies):
        for copy in copies:
            copy.wait_recv()

    def halo_copies(ref, base):
        def halo(src, dst, i, where):
            return remote(ref.at[src], ref.at[dst], halo_send, halo_recv, base + i, base + i, where)

        return (
            (up, [halo(pl.ds(0, 2), pl.ds(6, 2), 0, x_lo)]),
            (down, [halo(pl.ds(2, 2), pl.ds(4, 2), 1, x_hi)]),
            (left, [halo(0, 10, 2, y_lo), halo(2, 11, 3, y_lo)]),
            (right, [halo(1, 8, 4, y_hi), halo(3, 9, 5, y_hi)]),
        )

    halos = [halo_copies(kx, 0), halo_copies(vx, 6)]

    def start_halos(which):
        for there, copies in halos[which]:
            pl.when(there)(lambda copies=copies: start_all(copies))

    def halos_arrive(which, ref, fill):
        flat = [copy for _, copies in halos[which] for copy in copies]
        for there, index, slot in ((up, [1], 4), (down, [0], 6), (left, [4, 5], 8), (right, [2, 3], 10)):

            def arrive(index=index):
                wait_recvs([flat[i] for i in index])

            def outside(slot=slot):
                ref[slot : slot + 2] = fill

            pl.when(there)(arrive)
            pl.when(jnp.logical_not(there))(outside)

    pools = (pool_k, pool_v)
    started = ([], [])

    def pooled_copy(which, chip, part, i, where):
        block = pools[which].at[chip, part]
        base = n_y * which
        return remote(block, block, pool_send, pool_recv, base + i, base + 2 * chip + part, where)

    def send_pooled(which, chip, where):
        copy = pooled_copy(which, chip, core, len(started[which]), where)
        copy.start()
        started[which].append(copy)

    def pass_on(which):
        for chip in reversed(others):
            pooled_copy(which, chip, core, 0, sibling).wait_recv()
            send_pooled(which, chip, sibling)

    def handed(which):
        for chip in [z] + others:
            pooled_copy(which, chip, 1 - core, 0, sibling).wait_recv()

    for which in range(2):
        for chip in others:
            send_pooled(which, z, {"sy": 2 * chip + core})
        start_halos(which)
    for which in range(2):
        send_pooled(which, z, sibling)

    def turn_keys(w, b, block):
        pad = jnp.zeros((48, WIN), BF)
        kt[w, pl.ds(WIN * b, WIN), :] = jnp.concatenate([block, pad], 0).T

    def turn_values(w, b, block):
        pad = jnp.zeros((64, WIN), BF)
        vt[w, pl.ds(WIN * b, WIN), :] = jnp.concatenate([block, pad], 0).T

    for copy in reads[3:]:
        copy.wait()
    for w in range(4):
        kk[w, 0] = kx[w]
        vv[w, 0] = vx[w]
        turn_keys(w, 0, kx[w])
        turn_values(w, 0, vx[w])

    def rows_of(ref, w, part, p):
        first, last = PARTS[part]
        return jnp.concatenate(
            [ref[w, b, 64 * p : 64 * p + 64, :] for b in range(first, last)], 1
        )

    def span(part):
        first, last = PARTS[part]
        return slice(WIN * first, WIN * last)

    every = [(w, p) for w in range(4) for p in range(PAIRS)]

    def head(ref, w, h):
        return ref[w, 32 * h : 32 * h + 32, :]

    def score(part):
        one_row = jnp.where(iota((16, 256), 0) == 0, 1.0, 0.0).astype(BF)
        at = span(part)
        for w in range(4):
            pairs = [diagonal(head(q_ref, w, 2 * p), head(q_ref, w, 2 * p + 1)) for p in range(PAIRS)]
            scores = [dot(kt[w, at, :], placed(pairs[p], p, one_row)) for p in range(PAIRS)]
            tops = [jnp.max(x, axis=0, keepdims=True) for x in scores]
            lows = [jnp.exp2((x - top) * EXPC).astype(BF) for x, top in zip(scores, tops)]
            for p in range(PAIRS):
                e_s[w, p, at, :] = lows[p]
                m_s[w, p, part] = jnp.broadcast_to(tops[p], (8, 256))

    def weigh(part):
        ones = jnp.ones((16, WIN * (PARTS[part][1] - PARTS[part][0])), BF)
        for w, p in every:
            rows = jnp.concatenate([rows_of(vv, w, part, p), ones], 0)
            a_s[w, p, part] = dot(rows, e_s[w, p, span(part), :])

    score(0)
    weigh(0)

    for w in range(4):
        r, c = divmod(w, 2)
        mixed = dot(ow_ref[...], go_ref[w])
        mixed = jnp.where(iota((FEAT, WIN), 1) < GRP * cnt_ref[r, c], mixed, 0.0)
        gm[w] = mixed.astype(BF)
    owt[...] = ow_ref[...].T

    def beside_slot(w, s):
        r, c = divmod(w, 2)
        n0, n1, n2, n3 = neighbours(w)
        code = adj_ref[r, c, s]
        return jnp.where(code < 2, jnp.where(code == 0, n0, n1), jnp.where(code == 2, n2, n3))

    def listed(which, w):
        r, c = divmod(w, 2)
        far = [far_ref[r, c, f] for f in range(4)]
        return jnp.concatenate([unpack(pools[which][e // 2, e % 2]) for e in far], 0).T

    pass_on(0)
    halos_arrive(0, kx, jnp.where(iota((2, AUG, WIN), 1) == FEAT, MASKED, 0.0).astype(BF))
    for w in range(4):
        for s in range(2):
            block = kx[beside_slot(w, s)]
            kk[w, 1 + s] = block
            turn_keys(w, 1 + s, block)
    score(1)

    handed(0)
    for w in range(4):
        rows = listed(0, w)
        bad = (iota((16, WIN), 0) == 0) & (rows[:16].astype(F32) > 0.5 * MARK)
        block = jnp.concatenate([rows, jnp.where(bad, MASKED, 0.0).astype(BF)], 0)
        kk[w, 3] = block
        turn_keys(w, 3, block)
    pass_on(1)
    score(2)

    halos_arrive(1, vx, jnp.zeros((2, FEAT, WIN), BF))
    for w in range(4):
        for s in range(2):
            block = vx[beside_slot(w, s)]
            vv[w, 1 + s] = block
            turn_values(w, 1 + s, block)
    weigh(1)
    handed(1)
    for w in range(4):
        block = listed(1, w)
        vv[w, 3] = block
        turn_values(w, 3, block)
    weigh(2)

    for w, p in every:
        keep = GRP * cnt_ref[w // 2, w % 2]
        tops = [m_s[w, p, i, 0:1, :] for i in range(3)]
        top = jnp.maximum(jnp.maximum(tops[0], tops[1]), tops[2])
        shares = [jnp.exp2((t - top) * EXPC) for t in tops]
        total = sum(share * a_s[w, p, i] for i, share in enumerate(shares))
        inverse = 1.0 / total[64:65]
        first = total[:32, :WIN] * inverse[:, :WIN]
        second = total[32:64, WIN:] * inverse[:, WIN:]
        both = jnp.concatenate([first, second], 0)
        product = both * gm[w, 64 * p : 64 * p + 64, :].astype(F32)
        centre = jnp.concatenate(
            [
                jnp.sum(product[:32], axis=0, keepdims=True),
                jnp.sum(product[32:], axis=0, keepdims=True),
            ],
            1,
        )
        c_s[w, p] = jnp.broadcast_to(centre, (8, 256))
        for i, share in enumerate(shares):
            f_s[w, p, i] = jnp.broadcast_to(share * inverse, (8, 256))
        both = jnp.where(iota((64, WIN), 1) < keep, both, 0.0)
        att[w, 64 * p : 64 * p + 64, :] = both.astype(BF)

    def scaled_heads(ref, w, p, factor):
        return diagonal(
            (head(ref, w, 2 * p).astype(F32) * factor[:, :WIN]).astype(BF),
            (head(ref, w, 2 * p + 1).astype(F32) * factor[:, WIN:]).astype(BF),
        )

    def value_terms(part):
        at = span(part)
        for w, p in every:
            rows = scaled_heads(gm, w, p, f_s[w, p, part, 0:1, :])
            g_s[w, FEAT + 64 * p : FEAT + 64 * p + 64, at] = dot_nt(rows, e_s[w, p, at, :])

    def key_terms(part):
        no_row = jnp.zeros((16, 256), BF)
        at = span(part)
        for w in range(4):
            slopes, backs, terms = [], [], []
            lows = [e_s[w, p, at, :] for p in range(PAIRS)]
            olds = [gq_s[w, 64 * p : 64 * p + 64, :] for p in range(PAIRS)]
            for p in range(PAIRS):
                pair = diagonal(head(gm, w, 2 * p), head(gm, w, 2 * p + 1))
                prob = dot(vt[w, at, :], placed(pair, p, no_row))
                slopes.append((lows[p].astype(F32) * (prob - c_s[w, p, 0:1, :])).astype(BF))
            for p in range(PAIRS):
                scaled = f_s[w, p, part, 0:1, :] * SCALE
                back = dot(rows_of(kk, w, part, p), slopes[p]) * scaled
                backs.append(jnp.concatenate([back[:32, :WIN], back[32:, WIN:]], 0))
                terms.append(dot_nt(scaled_heads(q_ref, w, p, scaled), slopes[p]))
            for p in range(PAIRS):
                rows = slice(64 * p, 64 * p + 64)
                back = backs[p] if part == 2 else backs[p] + olds[p]
                if part == 0:
                    gq_ref[w, rows, :] = back.astype(BF)
                else:
                    gq_s[w, rows, :] = back
                g_s[w, rows, at] = terms[p]

    entries = 32 * n_y
    chosen = []
    for w in range(4):
        row, lane = iota((entries, WIN), 0), iota((entries, WIN), 1)
        want = jnp.zeros((entries, WIN), jnp.int32)
        for f in range(4):
            code = far_ref[w // 2, w % 2, f]
            want = jnp.where(lane // 32 == f, 32 * code + lane - 32 * f, want)
        chosen.append(jnp.where(row == want, 1.0, 0.0).astype(BF))

    def half_copy(which):
        return remote(
            pg_out.at[which, :, 1 - core], pg_half.at[which], half_send, half_recv, which, which, sibling
        )

    def send_half(which):
        spread = None
        for w in range(4):
            term = dot_nt(chosen[w], g_s[w, FEAT * which : FEAT * which + FEAT, 3 * WIN :].astype(BF))
            spread = term if spread is None else spread + term
        spread = pack(spread.reshape(n_y, 32, FEAT)).astype(BF)
        pg_out[which] = spread.reshape(n_z, 2, 48, WIN)
        half_copy(which).start()

    def pg_copy(which, i, src, dst, where):
        i, j = n_z * which + i, n_z * which + dst
        return remote(pg_sum.at[which, src], pg_in.at[which, dst], pg_send, pg_recv, i, j, where)

    def pg_sends(which):
        return [
            pg_copy(which, i, chip_at(step), z, {"sy": 2 * chip_at(step) + core})
            for i, step in enumerate(steps)
        ]

    def send_owners(which):
        half_copy(which).wait_recv()
        both = pg_out[which, :, core].astype(F32) + pg_half[which].astype(F32)
        pg_sum[which] = both.astype(BF)
        start_all(pg_sends(which))

    def toward(w, code, which):
        r, c = divmod(w, 2)
        total = None
        for s in range(2):
            here = (adj_ref[r, c, s] == code).astype(F32)
            term = g_s[w, FEAT * which : FEAT * which + FEAT, (1 + s) * WIN : (2 + s) * WIN] * here
            total = term if total is None else total + term
        return total

    def rims(which):
        def rim(src, dst, i, where):
            rows = pl.ds(FEAT * which, FEAT)
            i = 4 * which + i
            return remote(
                rim_out.at[pl.ds(src, 2), rows],
                rim_in.at[pl.ds(dst, 2), rows],
                rim_send,
                rim_recv,
                i,
                i,
                where,
            )

        return (
            (up, rim(0, 2, 0, x_lo)),
            (down, rim(2, 0, 1, x_hi)),
            (left, rim(4, 6, 2, y_lo)),
            (right, rim(6, 4, 3, y_hi)),
        )

    def send_rims(which):
        at = slice(FEAT * which, FEAT * which + FEAT)
        for w in range(4):
            r, c = divmod(w, 2)
            rim_out[2 * r + c, at] = toward(w, r, which).astype(BF)
            rim_out[4 + 2 * c + r, at] = toward(w, 2 + c, which).astype(BF)
        for there, copy in rims(which):
            pl.when(there)(copy.start)

    value_terms(2)
    send_half(1)

    mine = pl.ds(pl.multiple_of(hd * FEAT, FEAT), FEAT)
    theirs = pl.ds(pl.multiple_of((1 - hd) * FEAT, FEAT), FEAT)
    for w in range(4):
        bo_out[w] = dot(owt[theirs, :], att[w]).astype(BF)
    share = remote(bo_out, bo_in, bo_send, bo_recv, 0, 0, partner)
    share.start()

    value_terms(1)
    send_rims(1)
    send_owners(1)
    key_terms(2)
    send_half(0)
    value_terms(0)
    send_owners(0)
    key_terms(1)
    send_rims(0)
    key_terms(0)

    writes = [
        pltpu.make_async_copy(src, dst, out_sem.at[i])
        for i, (src, dst) in enumerate(
            ((gq_ref, gq_out_ref), (bo_ref, bo_out_ref), (gk_ref, gk_out_ref), (gv_ref, gv_out_ref))
        )
    ]
    writes[0].start()

    for w in range(4):
        bo_own[w] = dot(owt[mine, :], att[w])

    share.wait_recv()
    for w in range(4):
        bo_ref[w] = (bo_own[w] + bo_in[w].astype(F32)).astype(BF)
    writes[1].start()

    for which in (1, 0):
        at = slice(FEAT * which, FEAT * which + FEAT)
        for there, i, slot in ((up, 1, 0), (down, 0, 2), (left, 3, 4), (right, 2, 6)):

            def none(slot=slot, at=at):
                rim_in[slot : slot + 2, at] = jnp.zeros((2, FEAT, WIN), BF)

            pl.when(there)(rims(which)[i][1].wait_recv)
            pl.when(jnp.logical_not(there))(none)

        for step in steps:
            pg_copy(which, 0, chip_at(step), chip_at(step), sibling).wait_recv()
        coarse = pg_sum[which, z].astype(F32)
        for step in steps:
            coarse = coarse + pg_in[which, chip_at(step)].astype(F32)
        coarse = (unpack(coarse) * (1.0 / GRP)).T.astype(BF)
        for w in range(4):
            r, c = divmod(w, 2)
            total = g_s[w, at, :WIN] + toward(w ^ 2, r, which) + toward(w ^ 1, 2 + c, which)
            total = total + rim_in[2 * r + c, at].astype(F32)
            total = total + rim_in[4 + 2 * c + r, at].astype(F32)
            row, lane = iota((32, WIN), 0), iota((32, WIN), 1)
            member = jnp.where(row == 8 * w + lane // GRP, 1.0, 0.0).astype(BF)
            total = total + dot(coarse, member)
            (gv_ref if which else gk_ref)[w] = total.astype(BF)
        writes[2 + which].start()

    for which in range(2):
        for there, copies in halos[which]:
            pl.when(there)(lambda copies=copies: wait_sends(copies))
        wait_sends(started[which])
        half_copy(which).wait_send()
        wait_sends(pg_sends(which))
        for there, copy in rims(which):
            pl.when(there)(copy.wait_send)
    share.wait_send()
    for copy in writes:
        copy.wait()


def hand_over(*refs):
    given, out, held, sems = refs[:4], refs[4:8], refs[8:12], refs[12]
    reads = [pltpu.make_async_copy(given[i], held[i], sems.at[i]) for i in range(4)]
    writes = [pltpu.make_async_copy(held[i], out[i], sems.at[4 + i]) for i in range(4)]
    for copy in reads:
        copy.start()
    for read, write in zip(reads, writes):
        read.wait()
        write.start()
    for copy in writes:
        copy.wait()


def local(n_x, n_y, queries, key_field, value_field, grad_output, out_weight, counts, adjacent, far_list):
    def flat(x):
        return x.reshape(4, -1, WIN)

    hbm = pl.BlockSpec(memory_space=pl.ANY)
    shape = jax.ShapeDtypeStruct((4, FEAT, WIN), BF)
    dma = pltpu.SemaphoreType.DMA
    outs = pl.pallas_call(
        lambda *refs: kernel(n_x, n_y, *refs),
        out_shape=[shape] * 4,
        in_specs=[hbm] * 8,
        out_specs=[hbm] * 4,
        scratch_shapes=[
            pltpu.SMEM(counts.shape, jnp.int32),
            pltpu.SMEM(adjacent.shape, jnp.int32),
            pltpu.SMEM(far_list.shape, jnp.int32),
            pltpu.VMEM((4, FEAT, WIN), BF),
            pltpu.VMEM((4, 2 * FEAT, WIN), BF),
            pltpu.VMEM((FEAT, 2 * FEAT), BF),
            pltpu.VMEM((4, FEAT, WIN), BF),
            pltpu.VMEM((4, FEAT, WIN), BF),
            pltpu.VMEM((4, FEAT, WIN), BF),
            pltpu.VMEM((4, FEAT, WIN), BF),
            pltpu.VMEM((12, AUG, WIN), BF),
            pltpu.VMEM((12, FEAT, WIN), BF),
            pltpu.VMEM((4, 4, AUG, WIN), BF),
            pltpu.VMEM((4, 4, FEAT, WIN), BF),
            pltpu.VMEM((4, 512, 256), BF),
            pltpu.VMEM((4, 512, 256), BF),
            pltpu.VMEM((n_y // 2, 2, 48, WIN), BF),
            pltpu.VMEM((n_y // 2, 2, 48, WIN), BF),
            pltpu.VMEM((4, FEAT, WIN), BF),
            pltpu.VMEM((2 * FEAT, FEAT), BF),
            pltpu.VMEM((4, PAIRS, 512, 256), BF),
            pltpu.VMEM((4, PAIRS, 3, 8, 256), F32),
            pltpu.VMEM((4, PAIRS, 3, 80, 256), F32),
            pltpu.VMEM((4, PAIRS, 3, 8, 256), F32),
            pltpu.VMEM((4, PAIRS, 8, 256), F32),
            pltpu.VMEM((4, FEAT, WIN), BF),
            pltpu.VMEM((4, FEAT, WIN), F32),
            pltpu.VMEM((4, 2 * FEAT, 512), F32),
            pltpu.VMEM((2, n_y // 2, 2, 48, WIN), BF),
            pltpu.VMEM((2, n_y // 2, 48, WIN), BF),
            pltpu.VMEM((2, n_y // 2, 48, WIN), BF),
            pltpu.VMEM((2, n_y // 2, 48, WIN), BF),
            pltpu.VMEM((8, 2 * FEAT, WIN), BF),
            pltpu.VMEM((8, 2 * FEAT, WIN), BF),
            pltpu.VMEM((4, FEAT, WIN), BF),
            pltpu.VMEM((4, FEAT, WIN), BF),
            pltpu.VMEM((4, FEAT, WIN), F32),
            dma((12,)),
            dma((12,)),
            dma((2 * n_y,)),
            dma((2 * n_y,)),
            dma((8,)),
            dma((8,)),
            dma((n_y,)),
            dma((n_y,)),
            dma((2,)),
            dma((2,)),
            dma((1,)),
            dma((1,)),
            dma((8,)),
            dma((4,)),
        ],
        compiler_params=pltpu.CompilerParams(
            collective_id=0, has_side_effects=True, vmem_limit_bytes=VMEM
        ),
    )(flat(queries), flat(key_field), flat(value_field), flat(grad_output), out_weight, counts, adjacent, far_list)
    block_out, grad_queries, grad_keys, grad_values = pl.pallas_call(
        hand_over,
        out_shape=[shape] * 4,
        in_specs=[hbm] * 4,
        out_specs=[hbm] * 4,
        scratch_shapes=[pltpu.VMEM((4, FEAT, WIN), BF)] * 4 + [dma((8,))],
        compiler_params=pltpu.CompilerParams(vmem_limit_bytes=VMEM),
    )(*outs)
    return (
        block_out.reshape(2, 2, FEAT, WIN),
        grad_queries.reshape(queries.shape),
        grad_keys.reshape(queries.shape),
        grad_values.reshape(queries.shape),
    )


def solution(mesh):
    n_x, n_y = mesh.shape["sx"], mesh.shape["sy"]
    grid = P("sx", "sy")
    heads = P("sx", "sy", "hd", None, None)
    return jax.shard_map(
        lambda *args: local(n_x, n_y, *args),
        mesh=mesh,
        in_specs=(heads, heads, heads, grid, P("hd", None), grid, grid, grid),
        out_specs=(P("sx", "sy", "hd", None), heads, heads, heads),
        check_vma=False,
    )
```

time: 42.2 us -> 34.9 us (0.83); the launches traced: 42.1 us -> 34.3 us
  Pallas kernels: 41.4 us -> 33.7 us
    pallas_call x1, Pallas kernels: 39.3 us -> 31.7 us  [local(): pl.pallas_call(lambda *refs: kernel(n_x, n_y, *refs), out_shape=[shape] *...]
where the time goes in v3:
time: 34.9 us; the launch traced here: 34.3 us
  Pallas kernels  33.7 us (97%)
  between operations  0.64 us (2%)
    pallas_call x1, Pallas kernels, local(): pl.pallas_call(lambda *refs: kernel(n_x, n_y, *refs), out_shape=[shape] *...  31.7 us
    pallas_call x1, Pallas kernels, local(): pl.pallas_call(hand_over, out_shape=[shape] * 4, in_specs=[hbm] * 4, out_...  1.97 us

profile of v3, /device:TPU:1, one launch (start us, length us, event | category | flops | bytes accessed | tf_op | source)
XLA Modules:
  0.0 34.3 jit_solution(7540197775920234717)
XLA Ops:
  0.6 31.7 %shard_map.111 = (bf16[4,192,128]{2,1,0:T(8,128)(2,1)}, bf16[4,192,128]{2,1,0:T(8,128)(2,1)}, bf16[4,192,128]{2,1,0:T(8,128)(2,1)}, bf16[4,192,128]{2,1,0:T(8,128)(2,1)}) custom-call(bf16[4,192,128]{2,1,0:T(8,128)(2,1)} %bitcast.9, bf16[4,192,128]{2,1,0:T(8,128)(2,1)} %bitcast.10, bf16[4,192,128]{2,1,0:T(8,128)(2,1)} %bitcast.11, ...), custom_call_target="tpu_custom_call" | custom-call | tf_op jit(solution)/shard_map/pallas_call | solution.py:631
  32.3 2.0 %shard_map.112 = (bf16[4,192,128]{2,1,0:T(8,128)(2,1)}, bf16[4,192,128]{2,1,0:T(8,128)(2,1)}, bf16[4,192,128]{2,1,0:T(8,128)(2,1)}, bf16[4,192,128]{2,1,0:T(8,128)(2,1)}) custom-call(bf16[4,192,128]{2,1,0:T(8,128)(2,1)} %get-tuple-element.12.refs_0_, bf16[4,192,128]{2,1,0:T(8,128)(2,1)} %get-tuple-element.13.refs_1_, ...), custom_call_target="tpu_custom_call" | custom-call | tf_op jit(solution)/shard_map/pallas_call | solution.py:693

commit v4 on v3

--- a/solution.py
+++ b/solution.py
@@ -43,13 +43,9 @@
     )
 
 
-def placed(pair, p, tail):
-    pieces = [pair]
-    if p > 0:
-        pieces = [jnp.zeros((64 * p, 256), BF)] + pieces
-    if p < PAIRS - 1:
-        pieces = pieces + [jnp.zeros((64 * (PAIRS - 1 - p), 256), BF)]
-    return jnp.concatenate(pieces + [tail, jnp.zeros((48, 256), BF)], 0)
+def stacked(*pieces):
+    rest = WIN - sum(piece.shape[0] for piece in pieces)
+    return jnp.concatenate(list(pieces) + ([jnp.zeros((rest, 256), BF)] if rest else []), 0)
 
 
 def neighbours(w):
@@ -290,11 +286,14 @@
 
     def turn_keys(w, b, block):
         pad = jnp.zeros((48, WIN), BF)
-        kt[w, pl.ds(WIN * b, WIN), :] = jnp.concatenate([block, pad], 0).T
+        for p in range(PAIRS):
+            rows = jnp.concatenate([block[64 * p : 64 * p + 64], block[FEAT:], pad], 0)
+            kt[w, p, pl.ds(WIN * b, WIN), :] = rows.T
 
     def turn_values(w, b, block):
         pad = jnp.zeros((64, WIN), BF)
-        vt[w, pl.ds(WIN * b, WIN), :] = jnp.concatenate([block, pad], 0).T
+        vt[w, 0, pl.ds(WIN * b, WIN), :] = block[:WIN].T
+        vt[w, 1, pl.ds(WIN * b, WIN), :] = jnp.concatenate([block[WIN:], pad], 0).T
 
     for copy in reads[3:]:
         copy.wait()
@@ -324,7 +323,7 @@
         at = span(part)
         for w in range(4):
             pairs = [diagonal(head(q_ref, w, 2 * p), head(q_ref, w, 2 * p + 1)) for p in range(PAIRS)]
-            scores = [dot(kt[w, at, :], placed(pairs[p], p, one_row)) for p in range(PAIRS)]
+            scores = [dot(kt[w, p, at, :], stacked(pairs[p], one_row)) for p in range(PAIRS)]
             tops = [jnp.max(x, axis=0, keepdims=True) for x in scores]
             lows = [jnp.exp2((x - top) * EXPC).astype(BF) for x, top in zip(scores, tops)]
             for p in range(PAIRS):
@@ -428,7 +427,7 @@
             g_s[w, FEAT + 64 * p : FEAT + 64 * p + 64, at] = dot_nt(rows, e_s[w, p, at, :])
 
     def key_terms(part):
-        no_row = jnp.zeros((16, 256), BF)
+        no_rows = jnp.zeros((64, 256), BF)
         at = span(part)
         for w in range(4):
             slopes, backs, terms = [], [], []
@@ -436,7 +435,8 @@
             olds = [gq_s[w, 64 * p : 64 * p + 64, :] for p in range(PAIRS)]
             for p in range(PAIRS):
                 pair = diagonal(head(gm, w, 2 * p), head(gm, w, 2 * p + 1))
-                prob = dot(vt[w, at, :], placed(pair, p, no_row))
+                pair = stacked(no_rows, pair) if p % 2 else stacked(pair)
+                prob = dot(vt[w, p // 2, at, :], pair)
                 slopes.append((lows[p].astype(F32) * (prob - c_s[w, p, 0:1, :])).astype(BF))
             for p in range(PAIRS):
                 scaled = f_s[w, p, part, 0:1, :] * SCALE
@@ -445,7 +445,7 @@
                 terms.append(dot_nt(scaled_heads(q_ref, w, p, scaled), slopes[p]))
             for p in range(PAIRS):
                 rows = slice(64 * p, 64 * p + 64)
-                back = backs[p] if part == 2 else backs[p] + olds[p]
+                back = backs[p] if part == 1 else backs[p] + olds[p]
                 if part == 0:
                     gq_ref[w, rows, :] = back.astype(BF)
                 else:
@@ -531,9 +531,6 @@
         for there, copy in rims(which):
             pl.when(there)(copy.start)
 
-    value_terms(2)
-    send_half(1)
-
     mine = pl.ds(pl.multiple_of(hd * FEAT, FEAT), FEAT)
     theirs = pl.ds(pl.multiple_of((1 - hd) * FEAT, FEAT), FEAT)
     for w in range(4):
@@ -541,15 +538,17 @@
     share = remote(bo_out, bo_in, bo_send, bo_recv, 0, 0, partner)
     share.start()
 
+    value_terms(2)
+    send_half(1)
     value_terms(1)
     send_rims(1)
     send_owners(1)
+    key_terms(1)
+    send_rims(0)
     key_terms(2)
     send_half(0)
     value_terms(0)
     send_owners(0)
-    key_terms(1)
-    send_rims(0)
     key_terms(0)
 
     writes = [
@@ -648,8 +647,8 @@
             pltpu.VMEM((12, FEAT, WIN), BF),
             pltpu.VMEM((4, 4, AUG, WIN), BF),
             pltpu.VMEM((4, 4, FEAT, WIN), BF),
-            pltpu.VMEM((4, 512, 256), BF),
-            pltpu.VMEM((4, 512, 256), BF),
+            pltpu.VMEM((4, PAIRS, 512, WIN), BF),
+            pltpu.VMEM((4, 2, 512, WIN), BF),
             pltpu.VMEM((n_y // 2, 2, 48, WIN), BF),
             pltpu.VMEM((n_y // 2, 2, 48, WIN), BF),
             pltpu.VMEM((4, FEAT, WIN), BF),

time: 34.9 us -> 34 us (0.974); the launches traced: 34.3 us -> 33.8 us
  Pallas kernels: 33.7 us -> 33.1 us
    pallas_call x1, Pallas kernels: 31.7 us -> 31.2 us  [local(): pl.pallas_call(lambda *refs: kernel(n_x, n_y, *refs), out_shape=[shape] *...]
where the time goes in v4:
time: 34 us; the launch traced here: 33.8 us
  Pallas kernels  33.1 us (97%)
  between operations  0.64 us (2%)
    pallas_call x1, Pallas kernels, local(): pl.pallas_call(lambda *refs: kernel(n_x, n_y, *refs), out_shape=[shape] *...  31.2 us
    pallas_call x1, Pallas kernels, local(): pl.pallas_call(hand_over, out_shape=[shape] * 4, in_specs=[hbm] * 4, out_...  1.97 us

profile of v4, /device:TPU:1, one launch (start us, length us, event | category | flops | bytes accessed | tf_op | source)
XLA Modules:
  0.0 33.8 jit_solution(15847062644162256812)
XLA Ops:
  0.6 31.2 %shard_map.111 = (bf16[4,192,128]{2,1,0:T(8,128)(2,1)}, bf16[4,192,128]{2,1,0:T(8,128)(2,1)}, bf16[4,192,128]{2,1,0:T(8,128)(2,1)}, bf16[4,192,128]{2,1,0:T(8,128)(2,1)}) custom-call(bf16[4,192,128]{2,1,0:T(8,128)(2,1)} %bitcast.9, bf16[4,192,128]{2,1,0:T(8,128)(2,1)} %bitcast.10, bf16[4,192,128]{2,1,0:T(8,128)(2,1)} %bitcast.11, ...), custom_call_target="tpu_custom_call" | custom-call | tf_op jit(solution)/shard_map/pallas_call | solution.py:630
  31.8 2.0 %shard_map.112 = (bf16[4,192,128]{2,1,0:T(8,128)(2,1)}, bf16[4,192,128]{2,1,0:T(8,128)(2,1)}, bf16[4,192,128]{2,1,0:T(8,128)(2,1)}, bf16[4,192,128]{2,1,0:T(8,128)(2,1)}) custom-call(bf16[4,192,128]{2,1,0:T(8,128)(2,1)} %get-tuple-element.12.refs_0_, bf16[4,192,128]{2,1,0:T(8,128)(2,1)} %get-tuple-element.13.refs_1_, ...), custom_call_target="tpu_custom_call" | custom-call | tf_op jit(solution)/shard_map/pallas_call | solution.py:692

commit v5 on v4

--- a/solution.py
+++ b/solution.py
@@ -104,6 +104,7 @@
     gm,
     owt,
     e_s,
+    prob_s,
     m_s,
     a_s,
     f_s,
@@ -336,6 +337,15 @@
             rows = jnp.concatenate([rows_of(vv, w, part, p), ones], 0)
             a_s[w, p, part] = dot(rows, e_s[w, p, span(part), :])
 
+    def grad_prob(w, p, at):
+        pair = diagonal(head(gm, w, 2 * p), head(gm, w, 2 * p + 1))
+        pair = stacked(jnp.zeros((64, 256), BF), pair) if p % 2 else stacked(pair)
+        return dot(vt[w, p // 2, at, :], pair)
+
+    def keep_prob(part):
+        for w, p in every:
+            prob_s[w, p, span(part), :] = grad_prob(w, p, span(part))
+
     score(0)
     weigh(0)
 
@@ -357,6 +367,7 @@
         far = [far_ref[r, c, f] for f in range(4)]
         return jnp.concatenate([unpack(pools[which][e // 2, e % 2]) for e in far], 0).T
 
+    keep_prob(0)
     pass_on(0)
     halos_arrive(0, kx, jnp.where(iota((2, AUG, WIN), 1) == FEAT, MASKED, 0.0).astype(BF))
     for w in range(4):
@@ -383,6 +394,7 @@
             vv[w, 1 + s] = block
             turn_values(w, 1 + s, block)
     weigh(1)
+    keep_prob(1)
     handed(1)
     for w in range(4):
         block = listed(1, w)
@@ -427,16 +439,13 @@
             g_s[w, FEAT + 64 * p : FEAT + 64 * p + 64, at] = dot_nt(rows, e_s[w, p, at, :])
 
     def key_terms(part):
-        no_rows = jnp.zeros((64, 256), BF)
         at = span(part)
         for w in range(4):
             slopes, backs, terms = [], [], []
             lows = [e_s[w, p, at, :] for p in range(PAIRS)]
             olds = [gq_s[w, 64 * p : 64 * p + 64, :] for p in range(PAIRS)]
             for p in range(PAIRS):
-                pair = diagonal(head(gm, w, 2 * p), head(gm, w, 2 * p + 1))
-                pair = stacked(no_rows, pair) if p % 2 else stacked(pair)
-                prob = dot(vt[w, p // 2, at, :], pair)
+                prob = grad_prob(w, p, at) if part == 2 else prob_s[w, p, at, :]
                 slopes.append((lows[p].astype(F32) * (prob - c_s[w, p, 0:1, :])).astype(BF))
             for p in range(PAIRS):
                 scaled = f_s[w, p, part, 0:1, :] * SCALE
@@ -542,9 +551,9 @@
     send_half(1)
     value_terms(1)
     send_rims(1)
-    send_owners(1)
     key_terms(1)
     send_rims(0)
+    send_owners(1)
     key_terms(2)
     send_half(0)
     value_terms(0)
@@ -654,6 +663,7 @@
             pltpu.VMEM((4, FEAT, WIN), BF),
             pltpu.VMEM((2 * FEAT, FEAT), BF),
             pltpu.VMEM((4, PAIRS, 512, 256), BF),
+            pltpu.VMEM((4, PAIRS, 384, 256), F32),
             pltpu.VMEM((4, PAIRS, 3, 8, 256), F32),
             pltpu.VMEM((4, PAIRS, 3, 80, 256), F32),
             pltpu.VMEM((4, PAIRS, 3, 8, 256), F32),

time: 34 us -> 34.4 us (1.012)
  Pallas kernels: 33.1 us -> 33.6 us
    pallas_call x1, Pallas kernels: 31.2 us -> 31.7 us  [local(): pl.pallas_call(lambda *refs: kernel(n_x, n_y, *refs), out_shape=[shape] *...]
where the time goes in v5:
time: 34.4 us; the launch traced here: 34.3 us
  Pallas kernels  33.6 us (98%)
  between operations  0.64 us (2%)
    pallas_call x1, Pallas kernels, local(): pl.pallas_call(lambda *refs: kernel(n_x, n_y, *refs), out_shape=[shape] *...  31.7 us
    pallas_call x1, Pallas kernels, local(): pl.pallas_call(hand_over, out_shape=[shape] * 4, in_specs=[hbm] * 4, out_...  1.97 us

profile of v5, /device:TPU:1, one launch (start us, length us, event | category | flops | bytes accessed | tf_op | source)
XLA Modules:
  0.0 34.3 jit_solution(7852174339504306556)
XLA Ops:
  0.6 31.7 %shard_map.111 = (bf16[4,192,128]{2,1,0:T(8,128)(2,1)}, bf16[4,192,128]{2,1,0:T(8,128)(2,1)}, bf16[4,192,128]{2,1,0:T(8,128)(2,1)}, bf16[4,192,128]{2,1,0:T(8,128)(2,1)}) custom-call(bf16[4,192,128]{2,1,0:T(8,128)(2,1)} %bitcast.9, bf16[4,192,128]{2,1,0:T(8,128)(2,1)} %bitcast.10, bf16[4,192,128]{2,1,0:T(8,128)(2,1)} %bitcast.11, ...), custom_call_target="tpu_custom_call" | custom-call | tf_op jit(solution)/shard_map/pallas_call | solution.py:639
  32.3 2.0 %shard_map.112 = (bf16[4,192,128]{2,1,0:T(8,128)(2,1)}, bf16[4,192,128]{2,1,0:T(8,128)(2,1)}, bf16[4,192,128]{2,1,0:T(8,128)(2,1)}, bf16[4,192,128]{2,1,0:T(8,128)(2,1)}) custom-call(bf16[4,192,128]{2,1,0:T(8,128)(2,1)} %get-tuple-element.12.refs_0_, bf16[4,192,128]{2,1,0:T(8,128)(2,1)} %get-tuple-element.13.refs_1_, ...), custom_call_target="tpu_custom_call" | custom-call | tf_op jit(solution)/shard_map/pallas_call | solution.py:702
